TPU v7x, 128 devices: a whole 4x4x4 slice. The times are simulated.
128 devices in a mesh: dp: 2 (over z_hi), expert: 64 (over y, z_lo, x, core).
Axes of the slice: x: 4, y: 4, z: 4 (z_hi: 2, z_lo: 2; z = z_hi * 2 + z_lo), core: 2. Of those that a mesh axis runs over, the one named last changes fastest.
Arguments:
- latent: bfloat16 [16384, 1024], P(('dp', 'expert')), may hold values from -6 to 6
- routes: int32 [16384, 8], P(('dp', 'expert')), may hold values from 0 to 63, all different within a row; in each aligned block of 128 rows (0 to 127, 128 to 255, ...) at most 20 rows name the same one
- gates: float32 [16384, 8], P(('dp', 'expert')), may hold values from 0.05 to 0.5
- grad_out: bfloat16 [16384, 4096], P(('dp', 'expert')), may hold values from -6 to 6
- w_out_t: bfloat16 [4096, 1024], P('expert'), may hold values from -0.1875 to 0.1875
- expert_up: bfloat16 [64, 1024, 2048], P('expert'), may hold values from -0.1875 to 0.1875
- expert_down: bfloat16 [64, 2048, 1024], P('expert'), may hold values from -0.125 to 0.125
Outputs:
- mixed: bfloat16 [16384, 4096], P(('dp', 'expert'))
- grad_latent: bfloat16 [16384, 1024], P(('dp', 'expert'))
- grad_w_out: float32 [4096, 1024], P('expert')
Inputs may be any that keep to these rules, and one draw needn't show every extreme that they name: `routes`: within the 128 rows of one device each row names 8 different experts, and no expert is named by more than 20 of those rows; some expert is named by exactly 20 rows of some device.
All inputs are finite; a program needn't handle non-finite values.
Results may differ from a plain program's by a relative error of at most 0.02.
Values may be sent and summed in bfloat16 or wider, within the bound.
A program may use at most 128 MiB of HBM per device.

v0:
```python
import jax
import jax.numpy as jnp
from jax import lax
from jax.sharding import PartitionSpec as P


def on_device(latent, routes, gates, grad_out, w_out_t, expert_up, expert_down):
    tok_rows = latent.shape[0]
    width = latent.shape[1]
    top_count = routes.shape[1]
    members = lax.axis_size("expert")
    local_experts = expert_up.shape[0]
    all_experts = members * local_experts
    capacity = max(4, tok_rows * top_count * 5 // (4 * all_experts))
    flat = routes.reshape(-1)
    onehot = (flat[:, None] == jnp.arange(all_experts, dtype=jnp.int32)[None, :]).astype(jnp.int32)
    before = jnp.cumsum(onehot, axis=0) - onehot
    slots = jnp.sum(before * onehot, axis=1)
    target = flat * capacity + slots
    repeated = jnp.repeat(latent, top_count, axis=0)
    outgoing = jnp.zeros((all_experts * capacity, width), jnp.bfloat16).at[target].set(repeated)
    outgoing = outgoing.reshape(members, local_experts, capacity, width)
    grad_cols = lax.all_to_all(grad_out, "expert", split_axis=1, concat_axis=0, tiled=True)
    full_weight = lax.all_gather(w_out_t, "expert", axis=0, tiled=True)
    grad_combined = jnp.dot(grad_out, full_weight, preferred_element_type=jnp.float32).astype(
        jnp.bfloat16
    )
    scaled = (
        jnp.repeat(grad_combined, top_count, axis=0).astype(jnp.float32) * gates.reshape(-1, 1)
    ).astype(jnp.bfloat16)
    grad_send = jnp.zeros((all_experts * capacity, width), jnp.bfloat16).at[target].set(scaled)
    grad_send = grad_send.reshape(members, local_experts, capacity, width)
    pre = jnp.einsum(
        "secl,elh->sech",
        lax.all_to_all(outgoing, "expert", split_axis=0, concat_axis=0, tiled=True),
        expert_up,
        preferred_element_type=jnp.float32,
    )
    act = (jnp.maximum(pre, 0.0) ** 2).astype(jnp.bfloat16)
    result = jnp.einsum(
        "sech,ehl->secl", act, expert_down, preferred_element_type=jnp.float32
    ).astype(jnp.bfloat16)
    returned = lax.all_to_all(result, "expert", split_axis=0, concat_axis=0, tiled=True)
    grad_recv = lax.all_to_all(grad_send, "expert", split_axis=0, concat_axis=0, tiled=True)
    grad_act = jnp.einsum(
        "secl,ehl->sech", grad_recv, expert_down, preferred_element_type=jnp.float32
    )
    grad_pre = (grad_act * 2.0 * jnp.maximum(pre, 0.0)).astype(jnp.bfloat16)
    grad_rows = jnp.einsum(
        "sech,elh->secl", grad_pre, expert_up, preferred_element_type=jnp.float32
    ).astype(jnp.bfloat16)
    grad_back = lax.all_to_all(grad_rows, "expert", split_axis=0, concat_axis=0, tiled=True)
    picked = (
        returned.reshape(-1, width)[target].astype(jnp.float32).reshape(tok_rows, top_count, width)
    )
    combined = jnp.sum(picked * gates[:, :, None], axis=1).astype(jnp.bfloat16)
    mixed = lax.dot_general(
        combined, full_weight, (((1,), (1,)), ((), ())), preferred_element_type=jnp.float32
    ).astype(jnp.bfloat16)
    partial_grad = lax.dot_general(
        grad_cols,
        lax.all_gather(combined, "expert", axis=0, tiled=True),
        (((0,), (0,)), ((), ())),
        preferred_element_type=jnp.float32,
    )
    grad_w_out = lax.psum(partial_grad.astype(jnp.bfloat16), "dp").astype(jnp.float32)
    gathered = (
        grad_back.reshape(-1, width)[target].astype(jnp.float32).reshape(tok_rows, top_count, width)
    )
    grad_latent = jnp.sum(gathered, axis=1).astype(jnp.bfloat16)
    return (mixed, grad_latent, grad_w_out)


def solution(mesh):
    in_specs = (
        P(("dp", "expert"), None),
        P(("dp", "expert"), None),
        P(("dp", "expert"), None),
        P(("dp", "expert"), None),
        P("expert", None),
        P("expert", None, None),
        P("expert", None, None),
    )
    out_specs = (P(("dp", "expert"), None), P(("dp", "expert"), None), P("expert", None))
    return jax.shard_map(
        on_device, mesh=mesh, in_specs=in_specs, out_specs=out_specs, check_vma=False
    )
```

profile of v0, /device:TPU:7, one launch (start us, length us, event | category | flops | bytes accessed | tf_op | source)
XLA Modules:
  0.0 424.5 jit_solution(16319579178837480149)
XLA Ops:
  9.8 18.0 %reduce-window.6 = s32[64,8,128]{2,1,0:T(8,128)S(1)} reduce-window(s32[64,8,128]{2,1,0:T(8,128)S(1)} %fusion.37, s32[]{:T(128)} %constant.8.clone.1), window={size=1x1x128 pad=0_0x0_0x127_0}, to_apply=%region_0.0 | reduce-window | flops 8323072 | bytes 524292 | tf_op jit(solution)/shard_map/reduce-window
  28.5 7.1 %scatter_custom_fusion = bf16[1280,1024]{1,0:T(8,128)(2,1)} fusion(s32[1024]{0:T(1024)S(1)} %bitcast.91, bf16[]{:T(256)} %constant.6.clone.1, bf16[128,1024]{1,0:T(8,128)(2,1)S(1)} %copy-done), kind=kCustom, calls=%fused_computation.30 | custom fusion | bytes 2883586 | tf_op jit(solution)/shard_map/scatter | solution.py:21
  35.6 3.5 reshape.113
  39.1 55.8 %all_to_all.39 = bf16[64,1,20,1024]{3,2,1,0:T(8,128)(2,1)S(1)} all-to-all(bf16[64,1,20,1024]{3,2,1,0:T(8,128)(2,1)S(1)} %bitcast.85), channel_id=1, replica_groups=mesh['dp'=2,'expert'=64] {'expert'}, dimensions={0} | all-to-all | bytes 5242880 | tf_op jit(solution)/shard_map/all_to_all | solution.py:35
  94.9 6.3 %fusion.11 = f32[64,20,2048]{2,0,1:T(8,128)S(1)} fusion(bf16[1,1024,2048]{2,1,0:T(8,128)(2,1)S(1)} %copy-done.9, bf16[64,1,20,1024]{3,2,1,0:T(8,128)(2,1)S(1)} %all_to_all.39), kind=kOutput, calls=%fused_computation.20 | convolution fusion | flops 5368709120 | bytes 17301504 | tf_op jit(solution)/shard_map/secl,elh->sech/dot_general | solution.py:33
  101.2 5.8 %convert_bitcast_fusion.1 = bf16[64,1,20,1024]{3,0,2,1:T(8,128)(2,1)S(1)} fusion(bf16[1,2048,1024]{2,1,0:T(8,128)(2,1)S(1)} %copy-done.7, f32[64,20,2048]{2,0,1:T(8,128)S(1)} %fusion.11), kind=kOutput, calls=%fused_computation.27 | convolution fusion | flops 5377884160 | bytes 17301504 | tf_op jit(solution)/shard_map/sech,ehl->secl/dot_general | solution.py:40
  107.1 3.1 copy.30
  110.2 8.5 %all-to-all-start.1 = ((bf16[64,1,20,1024]{3,2,1,0:T(8,128)(2,1)}), bf16[64,1,20,1024]{3,2,1,0:T(8,128)(2,1)}, u32[]{:S(2)}, u32[]{:S(2)}) async-start(bf16[64,1,20,1024]{3,2,1,0:T(8,128)(2,1)} %copy.30), calls=%async_computation.1 | async-start | bytes 6291456 | tf_op jit(solution)/shard_map/all_to_all | solution.py:43
  119.4 42.3 %all-to-all-done.1 = bf16[64,1,20,1024]{3,2,1,0:T(8,128)(2,1)} async-done(((bf16[64,1,20,1024]{3,2,1,0:T(8,128)(2,1)}), bf16[64,1,20,1024]{3,2,1,0:T(8,128)(2,1)}, u32[]{:S(2)}, u32[]{:S(2)}) %all-to-all-start.1) | async-done | bytes 2621472 | tf_op jit(solution)/shard_map/all_to_all | solution.py:43
  161.7 3.6 reshape.117
  165.3 5.3 %gather_fusion = bf16[1024,1024]{1,0:T(8,128)(2,1)} fusion(bf16[1280,1024]{1,0:T(8,128)(2,1)S(1)} %reshape.117, s32[1024]{0:T(1024)S(1)} %broadcast_clamp_fusion), kind=kCustom, calls=%fused_computation | custom fusion | bytes 4198400 | tf_op jit(solution)/shard_map/gather | solution.py:54
  170.7 3.7 fusion.5
  174.5 3.1 all-gather.3.cloned.1.call-done
  177.7 4.6 %fusion.29 = f32[128,1024]{1,0:T(8,128)S(1)} fusion(bf16[128,4096]{1,0:T(8,128)(2,1)S(1)} %copy-done.4, bf16[4096,1024]{1,0:T(8,128)(2,1)} %all-gather.3.cloned.1.call-done), kind=kOutput, calls=%fused_computation.37 | convolution fusion | flops 1074003968 | bytes 9961472 | tf_op jit(solution)/shard_map/dot_general | solution.py:25
  182.3 7.5 %scatter_custom_fusion.1 = bf16[1280,1024]{1,0:T(8,128)(2,1)} fusion(s32[1024]{0:T(1024)S(1)} %bitcast.93, f32[1024]{0:T(1024)S(1)} %mul.58, f32[128,1024]{1,0:T(8,128)S(1)} %fusion.29, bf16[]{:T(256)} %constant.6.clone.1), kind=kCustom, calls=%fused_computation.28 | custom fusion | flops 2097152 | bytes 3149826 | tf_op jit(solution)/shard_map/scatter | solution.py:31
  189.8 3.5 reshape.118
  193.4 60.5 %all_to_all.40 = bf16[64,1,20,1024]{3,2,1,0:T(8,128)(2,1)S(1)} all-to-all(bf16[64,1,20,1024]{3,2,1,0:T(8,128)(2,1)S(1)} %bitcast.86), channel_id=1, replica_groups=mesh['dp'=2,'expert'=64] {'expert'}, dimensions={0} | all-to-all | bytes 5242880 | tf_op jit(solution)/shard_map/all_to_all | solution.py:44
  253.9 9.4 %fusion.7 = f32[64,20,2048]{2,0,1:T(8,128)} fusion(bf16[1,2048,1024]{2,1,0:T(8,128)(2,1)S(1)} %copy-done.8, bf16[64,1,20,1024]{3,2,1,0:T(8,128)(2,1)S(1)} %all_to_all.40), kind=kOutput, calls=%fused_computation.16 | convolution fusion | flops 5368709120 | bytes 17301504 | tf_op jit(solution)/shard_map/secl,ehl->sech/dot_general | solution.py:45
  263.3 10.7 %convert_bitcast_fusion = bf16[64,1,20,1024]{3,0,2,1:T(8,128)(2,1)S(1)} fusion(bf16[1,1024,2048]{2,1,0:T(8,128)(2,1)S(1)} %copy-done.10, f32[64,20,2048]{2,0,1:T(8,128)} %fusion.7, f32[64,20,2048]{2,0,1:T(8,128)} %copy-done.11), kind=kOutput, calls=%fused_computation.26 | convolution fusion | flops 5380505600 | bytes 27787264 | tf_op jit(solution)/shard_map/sech,elh->secl/dot_general | solution.py:49
  274.0 3.1 copy.35
  277.1 7.8 %all-to-all-start.3 = ((bf16[64,1,20,1024]{3,2,1,0:T(8,128)(2,1)}), bf16[64,1,20,1024]{3,2,1,0:T(8,128)(2,1)S(1)}, u32[]{:S(2)}, u32[]{:S(2)}) async-start(bf16[64,1,20,1024]{3,2,1,0:T(8,128)(2,1)} %copy.35), calls=%async_computation.3 | async-start | bytes 6291456 | tf_op jit(solution)/shard_map/all_to_all | solution.py:52
  284.9 2.3 copy.36
  287.2 47.5 %all-to-all-done.3 = bf16[64,1,20,1024]{3,2,1,0:T(8,128)(2,1)S(1)} async-done(((bf16[64,1,20,1024]{3,2,1,0:T(8,128)(2,1)}), bf16[64,1,20,1024]{3,2,1,0:T(8,128)(2,1)S(1)}, u32[]{:S(2)}, u32[]{:S(2)}) %all-to-all-start.3) | async-done | bytes 2621472 | tf_op jit(solution)/shard_map/all_to_all | solution.py:52
  334.7 12.2 %all-to-all-start.4 = ((bf16[128,64,64]{0,2,1:T(8,128)(2,1)}), bf16[128,64,64]{0,2,1:T(8,128)(2,1)}, u32[]{:S(2)}, u32[]{:S(2)}) async-start(bf16[128,64,64]{0,2,1:T(8,128)(2,1)} %bitcast.87), calls=%async_computation.4 | async-start | bytes 2097152 | tf_op jit(solution)/shard_map/all_to_all | solution.py:23
  347.2 7.3 %convolution_convert_fusion = bf16[128,4096]{1,0:T(8,128)(2,1)} fusion(bf16[128,1024]{1,0:T(8,128)(2,1)S(1)} %copy-done.5, bf16[4096,1024]{1,0:T(8,128)(2,1)} %all-gather.3.cloned.1.call-done), kind=kOutput, calls=%fused_computation.11 | convolution fusion | flops 1074266112 | bytes 9699328 | tf_op jit(solution)/shard_map/dot_general | solution.py:57
  354.5 3.6 reshape.120
  358.2 5.3 %gather_fusion.1 = bf16[1024,1024]{1,0:T(8,128)(2,1)} fusion(bf16[1280,1024]{1,0:T(8,128)(2,1)S(1)} %reshape.120, s32[1024]{0:T(1024)S(1)} %broadcast_clamp_fusion), kind=kCustom, calls=%fused_computation.1 | custom fusion | bytes 4198400 | tf_op jit(solution)/shard_map/gather | solution.py:68
  363.5 1.7 all-to-all-done.4
  365.2 10.2 %all-gather.5.cloned.1.call-done = bf16[8192,1024]{1,0:T(8,128)(2,1)} async-done(((bf16[128,1024]{1,0:T(8,128)(2,1)}), bf16[8192,1024]{1,0:T(8,128)(2,1)}) %all-gather.5.cloned.1.call-update) | async-done | bytes 16777232 | tf_op jit(solution)/shard_map/all_gather | solution.py:62
  375.4 9.8 %fusion.30 = bf16[64,1024]{1,0:T(8,128)(2,1)} fusion(bf16[8192,1024]{1,0:T(8,128)(2,1)} %all-gather.5.cloned.1.call-done, bf16[128,64,64]{0,2,1:T(8,128)(2,1)} %all-to-all-done.4), kind=kOutput, calls=%fused_computation.39 | convolution fusion | flops 1073807360 | bytes 17956864 | tf_op jit(solution)/shard_map/dot_general | solution.py:60
  385.2 2.1 bitcast_reduce_fusion
  387.4 28.8 %all-reduce.2.cloned.1.call-done = bf16[64,1024]{1,0:T(8,128)(2,1)} async-done(((bf16[64,1024]{1,0:T(8,128)(2,1)}), bf16[64,1024]{1,0:T(8,128)(2,1)}) %all-reduce.2.cloned.1.call-update) | async-done | bytes 131088 | tf_op jit(solution)/shard_map/psum | solution.py:66
  (49 shorter events, 5.9 us)
Async XLA Ops:
  7.2 21.3 %copy-start = (bf16[128,1024]{1,0:T(8,128)(2,1)S(1)}, bf16[128,1024]{1,0:T(8,128)(2,1)}, u32[]{:S(2)}) copy-start(bf16[128,1024]{1,0:T(8,128)(2,1)} %param.7) | copy-start | bytes 786436
  7.2 170.5 %all-gather.3.cloned.1.call-start = ((), (), s32[]{:S(2)}) async-start(), calls=%async_computation.5 | async-start | bytes 8519680 | tf_op jit(solution)/shard_map/all_gather | solution.py:24
  39.1 55.8 %copy-start.9 = (bf16[1,1024,2048]{2,1,0:T(8,128)(2,1)S(1)}, bf16[1,1024,2048]{2,1,0:T(8,128)(2,1)}, u32[]{:S(2)}) copy-start(bf16[1,1024,2048]{2,1,0:T(8,128)(2,1)} %param.12) | copy-start | bytes 12582916
  94.9 6.3 %copy-start.7 = (bf16[1,2048,1024]{2,1,0:T(8,128)(2,1)S(1)}, bf16[1,2048,1024]{2,1,0:T(8,128)(2,1)}, u32[]{:S(2)}) copy-start(bf16[1,2048,1024]{2,1,0:T(8,128)(2,1)} %param.13) | copy-start | bytes 12582916
  101.2 5.9 %copy-start.11 = (f32[64,20,2048]{2,0,1:T(8,128)}, f32[64,20,2048]{2,0,1:T(8,128)S(1)}, u32[]{:S(2)}) copy-start(f32[64,20,2048]{2,0,1:T(8,128)S(1)} %fusion.11) | copy-start | bytes 31457284
  110.2 9.1 %copy-start.6 = (f32[128,8]{0,1:T(8,128)S(1)}, f32[128,8]{0,1:T(8,128)}, u32[]{:S(2)}) copy-start(f32[128,8]{0,1:T(8,128)} %param.9) | copy-start | bytes 12292
  110.2 51.5 %all-to-all-start.1 = ((bf16[64,1,20,1024]{3,2,1,0:T(8,128)(2,1)}), bf16[64,1,20,1024]{3,2,1,0:T(8,128)(2,1)}, u32[]{:S(2)}, u32[]{:S(2)}) async-start(bf16[64,1,20,1024]{3,2,1,0:T(8,128)(2,1)} %copy.30), calls=%async_computation.1 | async-start | bytes 6291456 | tf_op jit(solution)/shard_map/all_to_all | solution.py:43
  118.7 256.7 %all-gather.5.cloned.1.call-start = ((), (), s32[]{:S(2)}) async-start(), calls=%async_computation.6 | async-start | bytes 17039360 | tf_op jit(solution)/shard_map/all_gather | solution.py:62
  170.7 7.0 %copy-start.4 = (bf16[128,4096]{1,0:T(8,128)(2,1)S(1)}, bf16[128,4096]{1,0:T(8,128)(2,1)}, u32[]{:S(2)}) copy-start(bf16[128,4096]{1,0:T(8,128)(2,1)} %param.10) | copy-start | bytes 3145732
  193.4 60.5 %copy-start.8 = (bf16[1,2048,1024]{2,1,0:T(8,128)(2,1)S(1)}, bf16[1,2048,1024]{2,1,0:T(8,128)(2,1)}, u32[]{:S(2)}) copy-start(bf16[1,2048,1024]{2,1,0:T(8,128)(2,1)} %param.13) | copy-start | bytes 12582916
  253.9 9.4 %copy-start.10 = (bf16[1,1024,2048]{2,1,0:T(8,128)(2,1)S(1)}, bf16[1,1024,2048]{2,1,0:T(8,128)(2,1)}, u32[]{:S(2)}) copy-start(bf16[1,1024,2048]{2,1,0:T(8,128)(2,1)} %param.12) | copy-start | bytes 12582916
  277.1 57.6 %all-to-all-start.3 = ((bf16[64,1,20,1024]{3,2,1,0:T(8,128)(2,1)}), bf16[64,1,20,1024]{3,2,1,0:T(8,128)(2,1)S(1)}, u32[]{:S(2)}, u32[]{:S(2)}) async-start(bf16[64,1,20,1024]{3,2,1,0:T(8,128)(2,1)} %copy.35), calls=%async_computation.3 | async-start | bytes 6291456 | tf_op jit(solution)/shard_map/all_to_all | solution.py:52
  284.9 62.3 %copy-start.5 = (bf16[128,1024]{1,0:T(8,128)(2,1)S(1)}, bf16[128,1024]{1,0:T(8,128)(2,1)}, u32[]{:S(2)}) copy-start(bf16[128,1024]{1,0:T(8,128)(2,1)} %fusion.5) | copy-start | bytes 786436
  334.7 12.4 %copy-start.2 = (bf16[64,1,20,1024]{3,2,1,0:T(8,128)(2,1)}, bf16[64,1,20,1024]{3,2,1,0:T(8,128)(2,1)S(1)}, u32[]{:S(2)}) copy-start(bf16[64,1,20,1024]{3,2,1,0:T(8,128)(2,1)S(1)} %all-to-all-done.3) | copy-start | bytes 7864324
  334.7 30.4 %all-to-all-start.4 = ((bf16[128,64,64]{0,2,1:T(8,128)(2,1)}), bf16[128,64,64]{0,2,1:T(8,128)(2,1)}, u32[]{:S(2)}, u32[]{:S(2)}) async-start(bf16[128,64,64]{0,2,1:T(8,128)(2,1)} %bitcast.87), calls=%async_computation.4 | async-start | bytes 2097152 | tf_op jit(solution)/shard_map/all_to_all | solution.py:23
  346.9 69.2 %all-reduce.2.cloned.1.call-start = ((), (), s32[]{:S(2)}) async-start(), calls=%async_computation.7 | async-start | bytes 262144 | tf_op jit(solution)/shard_map/psum | solution.py:66
  363.5 21.7 %copy-start.3 = (bf16[1024,1024]{1,0:T(8,128)(2,1)S(1)}, bf16[1024,1024]{1,0:T(8,128)(2,1)}, u32[]{:S(2)}) copy-start(bf16[1024,1024]{1,0:T(8,128)(2,1)} %gather_fusion.1) | copy-start | bytes 6291460
  375.4 42.4 %copy-start.1 = (bf16[128,1024]{1,0:T(8,128)(2,1)S(1)}, bf16[128,1024]{1,0:T(8,128)(2,1)}, u32[]{:S(2)}) copy-start(bf16[128,1024]{1,0:T(8,128)(2,1)} %param.7) | copy-start | bytes 786436
Sparse Core Ops, SparseCore 0:
  9.7 167.8 all-gather.2
  179.9 195.3 all-gather.4
  385.3 30.7 all-reduce.1
where the time goes:
time: 431 us; the launch traced here: 425 us
  waiting for transfers between devices  134 us (31%)
  blocking collectives  116 us (27%)
  matrix products  54 us (13%)
  local copies, waits for them, and re-layouts  42.4 us (10%)
  other arithmetic  34 us (8%)
  starting transfers between devices  29.3 us (7%)
  between operations  14.2 us (3%)
    all_to_all x1, blocking collectives, on_device(): lax.all_to_all(grad_send, 'expert', split_axis=0, concat_axis=0, tiled=True)  60.5 us
    all_to_all x1, blocking collectives, on_device(): lax.all_to_all(outgoing, 'expert', split_axis=0, concat_axis=0, tiled=True)  55.8 us
    all_to_all x1, waiting for transfers between devices, on_device(): lax.all_to_all(grad_rows, 'expert', split_axis=0, concat_axis=0, tiled=True)  47.5 us
    all_to_all x1, waiting for transfers between devices, on_device(): lax.all_to_all(result, 'expert', split_axis=0, concat_axis=0, tiled=True)  42.3 us
    psum x1, waiting for transfers between devices, on_device(): lax.psum(partial_grad.astype(jnp.bfloat16), 'dp').astype(jnp.float32)  28.8 us
    another operation x3, other arithmetic  18.2 us
    all_to_all x1, starting transfers between devices, on_device(): lax.all_to_all(grad_out, 'expert', split_axis=1, concat_axis=0, tiled=True)  12.2 us
    dot_general x1, matrix products, on_device(): jnp.einsum('sech,elh->secl', grad_pre, expert_up, preferred_element_type=...  10.7 us
  transfers between devices with their start and end apart: 6, of which 6 were waited for; matrix products, arithmetic and copies ran while one was open for 28% of the time, Pallas kernels for 0%

commit v1 on v0

v1 whole, which is shorter than its diff:
```python
import functools

import jax
import jax.numpy as jnp
from jax import lax
from jax.experimental import pallas as pl
from jax.experimental.pallas import tpu as pltpu
from jax.sharding import PartitionSpec as P

BF = jnp.bfloat16
F32 = jnp.float32
MESH = pl.DeviceIdType.MESH
STRIDE = 11
CHUNKS = 4
PER = 16
MAIN = 256
EXTRA = 64
ROWS = 320


def iota(shape, dim):
    return lax.broadcasted_iota(jnp.int32, shape, dim)


def dot(a, b, ca=1, cb=0):
    return lax.dot_general(a, b, (((ca,), (cb,)), ((), ())), preferred_element_type=F32)


def index_of(y, z, x, c):
    return ((y * 2 + z) * 4 + x) * 2 + c


def kernel(
    latent, routes, gates, w_own, grad_out, up_hbm, down_hbm,
    mixed, grad_latent, grad_w,
    s1, r1, o1, b1, s2, r2, o2, b2, up, down, relu, xc, acc, extra,
    go, wj, pgs, pgr, cb, mps, gwp, gwr, dps, dpr,
    sel, selt, p_send, pg_send, p_back, pg_back,
    a2a_ss, a2a_rs, w_ss, w_rs, go_ss, go_rs, pg_ss, pg_rs, cb_ss, cb_rs, mx_ss, mx_rs,
    gw_ss, gw_rs, dp_ss, dp_rs, loc,
):
    dp = lax.axis_index("dp")
    me = lax.axis_index("expert")
    y, z, x, c = me // 16, (me // 8) % 2, (me // 2) % 4, me % 2
    mine = z * 2 + c

    def partner(k, sign):
        off = (STRIDE * k) % 64
        oy, oz, ox, oc = off // 16, (off // 8) % 2, (off // 2) % 4, off % 2
        return index_of((y + sign * oy + 4) % 4, (z + oz) % 2, (x + sign * ox + 4) % 4, (c + oc) % 2)

    def member(d):
        m = (mine + d) % 4
        return m, index_of(y, m // 2, x, m % 2)

    def remote(src, dst, ss, rs, dev):
        return pltpu.make_async_remote_copy(src, dst, ss, rs, device_id=(dp, dev), device_id_type=MESH)

    barrier = pltpu.get_barrier_semaphore()

    def greet(k, carry):
        pl.semaphore_signal(barrier, inc=1, device_id=(dp, partner(k, 1)), device_id_type=MESH)
        return carry

    lax.fori_loop(1, 64, greet, 0)
    pl.semaphore_signal(barrier, inc=1, device_id=(1 - dp, me), device_id_type=MESH)
    up_copy = pltpu.make_async_copy(up_hbm.at[0], up, loc.at[0])
    down_copy = pltpu.make_async_copy(down_hbm.at[0], down, loc.at[1])
    up_copy.start()
    down_copy.start()

    r = routes[...]
    g = gates[...]
    lane = iota((128, 128), 1)
    hot = jnp.zeros((128, 128), F32)
    gate = jnp.zeros((128, 128), F32)
    for k in range(8):
        hit = r[:, k : k + 1] == lane
        hot = hot + jnp.where(hit, 1.0, 0.0)
        gate = gate + jnp.where(hit, g[:, k : k + 1], 0.0)
    lower = jnp.where(iota((128, 128), 0) > lane, 1.0, 0.0).astype(BF)
    count = dot(lower, hot.astype(BF))
    slot = jnp.where(hot > 0.5, count, 255.0)
    gate_hi = gate.astype(BF).astype(F32)
    gate_lo = (gate - gate_hi).astype(BF).astype(F32)

    def names(j):
        return jnp.where(j < 1024, j >> 4, (j - 1024) >> 2), jnp.where(j < 1024, j & 15, 16 + (j & 3))

    e_row, s_row = names(iota((1280, 128), 0))
    spread_t = jnp.where(e_row == iota((1280, 128), 1), 1.0, 0.0).astype(BF)
    hit_t = dot(spread_t, slot.T.astype(BF)) == s_row.astype(F32)
    p_send[...] = jnp.where(hit_t, 1.0, 0.0).astype(BF)
    pg_send[:, 0:128] = jnp.where(hit_t, dot(spread_t, gate_hi.T.astype(BF)), 0.0).astype(BF)
    pg_send[:, 128:256] = jnp.where(hit_t, dot(spread_t, gate_lo.T.astype(BF)), 0.0).astype(BF)
    e_col, s_col = names(iota((128, 1280), 1))
    spread = jnp.where(e_col == iota((128, 1280), 0), 1.0, 0.0).astype(BF)
    hit_b = dot(slot.astype(BF), spread) == s_col.astype(F32)
    p_back[...] = jnp.where(hit_b, 1.0, 0.0).astype(BF)
    pg_back[0:128, :] = jnp.where(hit_b, dot(gate_hi.astype(BF), spread), 0.0).astype(BF)
    pg_back[128:256, :] = jnp.where(hit_b, dot(gate_lo.astype(BF), spread), 0.0).astype(BF)
    i, j = iota((256, 256), 0), iota((256, 256), 1)
    sel[...] = jnp.where(((i & 63) >> 2) * 16 + (i >> 6) * 4 + (i & 3) == j, 1.0, 0.0).astype(BF)
    selt[...] = jnp.where(((j & 63) >> 2) * 16 + (j >> 6) * 4 + (j & 3) == i, 1.0, 0.0).astype(BF)

    def unpack(packed):
        rows = dot(sel[...], packed).astype(BF)
        return jnp.concatenate([rows[q * 64 : (q + 1) * 64] for q in range(4)], axis=1)

    def pack(rows):
        stacked = jnp.concatenate([rows[:, q * 256 : (q + 1) * 256] for q in range(4)], axis=0)
        return dot(selt[...], stacked).astype(BF)

    def main_rows(ci):
        return pl.ds(pl.multiple_of(ci * MAIN, MAIN), MAIN)

    def fill(pick, source, buffer):
        def body(ci, carry):
            buffer[main_rows(ci), 0:1024] = dot(pick[main_rows(ci), :], source).astype(BF)
            more = pick[pl.ds(pl.multiple_of(1024 + ci * EXTRA, EXTRA), EXTRA), :]
            buffer[main_rows(ci), 1024:1280] = pack(dot(more, source).astype(BF))
            return carry

        lax.fori_loop(0, CHUNKS, body, 0)

    def block(k):
        return pl.ds(pl.multiple_of(k * 16, 16), 16)

    def start_out(which, src, dst):
        def body(k, carry):
            to = partner(k, 1)
            remote(src.at[block(to)], dst.at[block(k)], a2a_ss.at[which], a2a_rs.at[which, k // PER], to).start()
            return carry

        lax.fori_loop(1, 64, body, 0)
        dst[0:16, :] = src[block(me), :]

    def start_back(which, src, dst, ci):
        def body(k, carry):
            to = partner(k, -1)
            remote(src.at[block(k)], dst.at[block(me)], a2a_ss.at[which], a2a_rs.at[which, k // PER], to).start()
            return carry

        lax.fori_loop(jnp.maximum(ci * PER, 1), ci * PER + PER, body, 0)

        @pl.when(ci == 0)
        def _():
            dst[block(me), :] = src[0:16, :]

    def arrived(which, ci, src, dst, first):
        rows = pl.ds(0, 240) if first else main_rows(ci)
        remote(src.at[rows], dst.at[rows], a2a_ss.at[which], a2a_rs.at[which, ci], me).wait_recv()

    def all_sent(which, src, dst):
        rows = pl.ds(0, 1008)
        remote(src.at[rows], dst.at[rows], a2a_ss.at[which], a2a_rs.at[which, 0], me).wait_send()

    fill(p_send, latent[...], s1)
    pl.semaphore_wait(barrier, 64)

    half = x // 2
    w_slot = y * 4 + (x % 2) * 2 + c

    def w_rows(s):
        return pl.ds(pl.multiple_of(s * 64, 64), 64)

    def w_copy(i):
        to = index_of((y + i // 4) % 4, z, (x + i % 4) % 4, half)
        return to, remote(w_own, wj.at[w_rows(w_slot)], w_ss.at[i], w_rs.at[w_slot], to)

    def w_start(i, carry):
        to, copy = w_copy(i)

        @pl.when(to != me)
        def _():
            copy.start()

        @pl.when(to == me)
        def _():
            wj[w_rows(w_slot), :] = w_own[...]

        return carry

    lax.fori_loop(0, 16, w_start, 0)

    def feats(m, part):
        return pl.ds(pl.multiple_of(part * 1024 + (m // 2) * 512 + (m % 2) * 256, 256), 256)

    def tokens(m):
        return pl.ds(pl.multiple_of(m * 128, 128), 128)

    own_go = []
    for part in range(4):
        cols = pl.ds(part * 256, 256)
        for d in range(1, 4):
            m, to = member(d)
            remote(grad_out.at[:, feats(m, part)], go.at[tokens(mine), cols], go_ss.at[d], go_rs.at[mine], to).start()
        copy = pltpu.make_async_copy(grad_out.at[:, feats(mine, part)], go.at[tokens(mine), cols], loc.at[2 + part])
        copy.start()
        own_go.append(copy)

    start_out(0, s1, r1)

    def w_wait(i, carry):
        fy, fx, fc = i // 4, half_of(i), i % 2
        src = index_of(fy, z, fx, fc)

        @pl.when(src != me)
        def _():
            remote(w_own, wj.at[w_rows(i)], w_ss.at[0], w_rs.at[i], me).wait_recv()

        return carry

    def half_of(i):
        return c * 2 + (i // 2) % 2

    lax.fori_loop(0, 16, w_wait, 0)
    for copy in own_go:
        copy.wait()
    for d in range(1, 4):
        m, _ = member(d)
        remote(go.at[tokens(m)], go.at[tokens(m)], go_ss.at[d], go_rs.at[m], me).wait_recv()

    def partial_gc(n, carry):
        cols = pl.ds(pl.multiple_of(n * 256, 256), 256)
        pgs[:, cols] = dot(go[...], wj[:, cols]).astype(BF)
        return carry

    lax.fori_loop(0, 4, partial_gc, 0)
    for d in range(1, 4):
        m, to = member(d)
        remote(pgs.at[tokens(m)], pgr.at[tokens(mine)], pg_ss.at[d], pg_rs.at[mine], to).start()
    pgr[tokens(mine), :] = pgs[tokens(mine), :]
    for d in range(1, 4):
        m, _ = member(d)
        remote(pgs.at[tokens(m)], pgr.at[tokens(m)], pg_ss.at[d], pg_rs.at[m], me).wait_recv()
    gc = sum(pgr[m * 128 : (m + 1) * 128, :].astype(F32) for m in range(4)).astype(BF)
    fill(pg_send, jnp.concatenate([gc, gc], axis=0), s2)
    start_out(2, s2, r2)

    up_copy.wait()
    down_copy.wait()

    def load(src, ci):
        xc[0:MAIN, :] = src[main_rows(ci), 0:1024]
        xc[MAIN:ROWS, :] = unpack(src[main_rows(ci), 1024:1280])

    def store(dst, ci):
        dst[main_rows(ci), 0:1024] = acc[0:MAIN, :].astype(BF)
        dst[main_rows(ci), 1024:1280] = pack(acc[MAIN:ROWS, :].astype(BF))

    def hidden(h):
        return pl.ds(pl.multiple_of(h * 512, 512), 512)

    def arrived_chunk(which, ci, src, dst):
        @pl.when(ci == 0)
        def _():
            arrived(which, 0, src, dst, True)

        @pl.when(ci > 0)
        def _():
            arrived(which, ci, src, dst, False)

    def forward(ci, carry):
        arrived_chunk(0, ci, s1, r1)
        load(r1, ci)
        acc[...] = jnp.zeros_like(acc)

        def step(h, inner):
            pos = jnp.maximum(dot(xc[...], up[:, hidden(h)]), 0.0)
            relu[ci, :, hidden(h)] = pos
            acc[...] += dot((pos * pos).astype(BF), down[hidden(h), :])
            return inner

        lax.fori_loop(0, 4, step, 0)
        store(o1, ci)
        start_back(1, o1, b1, ci)
        return carry

    lax.fori_loop(0, CHUNKS, forward, 0)

    def backward(ci, carry):
        arrived_chunk(2, ci, s2, r2)
        load(r2, ci)
        acc[...] = jnp.zeros_like(acc)

        def step(h, inner):
            grad = dot(xc[...], down[hidden(h), :], 1, 1) * 2.0 * relu[ci, :, hidden(h)]
            acc[...] += dot(grad.astype(BF), up[:, hidden(h)], 1, 1)
            return inner

        lax.fori_loop(0, 4, step, 0)
        store(o2, ci)
        start_back(3, o2, b2, ci)
        return carry

    lax.fori_loop(0, CHUNKS, backward, 0)

    def gather_back(which, src, dst):
        for ci in range(CHUNKS):
            arrived(which, ci, src, dst, ci == 0)

        def body(ci, carry):
            rows = pl.ds(pl.multiple_of(ci * EXTRA, EXTRA), EXTRA)
            extra[rows, :] = unpack(dst[main_rows(ci), 1024:1280])
            return carry

        lax.fori_loop(0, CHUNKS, body, 0)

    gather_back(1, o1, b1)
    both = dot(pg_back[:, 0:1024], b1[:, 0:1024]) + dot(pg_back[:, 1024:1280], extra[...])
    cb[tokens(mine), :] = (both[0:128] + both[128:256]).astype(BF)
    for d in range(1, 4):
        m, to = member(d)
        remote(cb.at[tokens(mine)], cb.at[tokens(mine)], cb_ss.at[d], cb_rs.at[mine], to).start()
    for d in range(1, 4):
        m, _ = member(d)
        remote(cb.at[tokens(m)], cb.at[tokens(m)], cb_ss.at[d], cb_rs.at[m], me).wait_recv()

    def gw_to(part, i):
        return index_of(part, z, c * 2 + i // 2, i % 2)

    def weight_grad(n, carry):
        part = (y + n) % 4
        cols = pl.ds(pl.multiple_of(part * 256, 256), 256)
        gwp[cols, :] = dot(go[:, cols], cb[...], 0, 0).astype(BF)
        for i in range(4):
            to = gw_to(part, i)
            rows = w_rows(part * 4 + i)
            from_here = w_rows(y * 4 + x)

            @pl.when(to != me)
            def _():
                remote(gwp.at[rows], gwr.at[from_here], gw_ss.at[part * 4 + i], gw_rs.at[y * 4 + x], to).start()

            @pl.when(to == me)
            def _():
                gwr[from_here, :] = gwp[rows, :]

        return carry

    lax.fori_loop(0, 4, weight_grad, 0)

    def mix(part, carry):
        rows = pl.ds(pl.multiple_of(part * 256, 256), 256)
        mps[:, rows] = dot(cb[...], wj[rows, :], 1, 1).astype(BF)
        for d in range(1, 4):
            m, to = member(d)
            remote(mps.at[tokens(m), rows], mixed.at[:, feats(mine, part)], mx_ss.at[d], mx_rs.at[mine], to).start()
        mixed[:, feats(mine, part)] = mps[tokens(mine), rows]
        return carry

    lax.fori_loop(0, 4, mix, 0)

    def gw_wait(i, carry):
        src = index_of(i // 4, z, i % 4, half)

        @pl.when(src != me)
        def _():
            remote(gwp.at[w_rows(i)], gwr.at[w_rows(i)], gw_ss.at[0], gw_rs.at[i], me).wait_recv()

        return carry

    lax.fori_loop(0, 16, gw_wait, 0)
    total = sum(gwr[i * 64 : (i + 1) * 64, :].astype(F32) for i in range(16))
    dps[...] = total.astype(BF)
    exchange = pltpu.make_async_remote_copy(
        dps, dpr, dp_ss.at[0], dp_rs.at[0], device_id=(1 - dp, me), device_id_type=MESH
    )
    exchange.start()

    gather_back(3, o2, b2)
    grad_latent[...] = (
        dot(p_back[:, 0:1024], b2[:, 0:1024]) + dot(p_back[:, 1024:1280], extra[...])
    ).astype(BF)

    exchange.wait()
    grad_w[...] = dps[...].astype(F32) + dpr[...].astype(F32)

    for d in range(1, 4):
        m, _ = member(d)
        whole = remote(mps.at[tokens(m)], mps.at[tokens(m)], mx_ss.at[d], mx_rs.at[m], me)
        whole.wait_recv()
        whole.wait_send()
        remote(go.at[tokens(m)], go.at[tokens(m)], go_ss.at[d], go_rs.at[m], me).wait_send()
        remote(pgs.at[tokens(m)], pgr.at[tokens(m)], pg_ss.at[d], pg_rs.at[m], me).wait_send()
        remote(cb.at[tokens(m)], cb.at[tokens(m)], cb_ss.at[d], cb_rs.at[m], me).wait_send()

    def last(i, carry):
        to, copy = w_copy(i)

        @pl.when(to != me)
        def _():
            copy.wait_send()

        @pl.when(gw_to(i // 4, i % 4) != me)
        def _():
            remote(gwp.at[w_rows(i)], gwr.at[w_rows(i)], gw_ss.at[i], gw_rs.at[i], me).wait_send()

        return carry

    lax.fori_loop(0, 16, last, 0)
    all_sent(0, s1, r1)
    all_sent(1, o1, b1)
    all_sent(2, s2, r2)
    all_sent(3, o2, b2)


def on_device(latent, routes, gates, grad_out, w_out_t, expert_up, expert_down):
    vm = pl.BlockSpec(memory_space=pltpu.VMEM)
    hbm = pl.BlockSpec(memory_space=pl.ANY)
    dma = pltpu.SemaphoreType.DMA
    buffers = [pltpu.VMEM((1024, 1280), BF)] * 8
    scratch = buffers + [
        pltpu.VMEM((1024, 2048), BF),
        pltpu.VMEM((2048, 1024), BF),
        pltpu.VMEM((CHUNKS, ROWS, 2048), F32),
        pltpu.VMEM((ROWS, 1024), BF),
        pltpu.VMEM((ROWS, 1024), F32),
        pltpu.VMEM((256, 1024), BF),
        pltpu.VMEM((512, 1024), BF),
        pltpu.VMEM((1024, 1024), BF),
        pltpu.VMEM((512, 1024), BF),
        pltpu.VMEM((512, 1024), BF),
        pltpu.VMEM((512, 1024), BF),
        pltpu.VMEM((512, 1024), BF),
        pltpu.VMEM((1024, 1024), BF),
        pltpu.VMEM((1024, 1024), BF),
        pltpu.VMEM((64, 1024), BF),
        pltpu.VMEM((64, 1024), BF),
        pltpu.VMEM((256, 256), BF),
        pltpu.VMEM((256, 256), BF),
        pltpu.VMEM((1280, 128), BF),
        pltpu.VMEM((1280, 256), BF),
        pltpu.VMEM((128, 1280), BF),
        pltpu.VMEM((256, 1280), BF),
        dma((4,)), dma((4, 4)),
        dma((16,)), dma((16,)),
        dma((4,)), dma((4,)),
        dma((4,)), dma((4,)),
        dma((4,)), dma((4,)),
        dma((4,)), dma((4,)),
        dma((16,)), dma((16,)),
        dma((1,)), dma((1,)),
        dma((6,)),
    ]
    return pl.pallas_call(
        kernel,
        out_shape=(
            jax.ShapeDtypeStruct((128, 4096), BF),
            jax.ShapeDtypeStruct((128, 1024), BF),
            jax.ShapeDtypeStruct((64, 1024), F32),
        ),
        in_specs=[vm, vm, vm, vm, hbm, hbm, hbm],
        out_specs=(vm, vm, vm),
        scratch_shapes=scratch,
        compiler_params=pltpu.CompilerParams(
            collective_id=0, has_side_effects=True, vmem_limit_bytes=62 * 1024 * 1024
        ),
        cost_estimate=pl.CostEstimate(flops=25_000_000_000, bytes_accessed=20_000_000, transcendentals=0),
        name="moe_layer",
    )(latent, routes, gates, w_out_t, grad_out, expert_up, expert_down)


def solution(mesh):
    rows = P(("dp", "expert"), None)
    return jax.shard_map(
        on_device,
        mesh=mesh,
        in_specs=(rows, rows, rows, rows, P("expert", None), P("expert", None, None), P("expert", None, None)),
        out_specs=(rows, rows, P("expert", None)),
        check_vma=False,
    )
```

time: 431 us -> 220 us (0.51); the launches traced: 425 us -> 220 us
  Pallas kernels: 0 us -> 211 us
  waiting for transfers between devices: 134 us -> 0 us
  blocking collectives: 116 us -> 0 us
  matrix products: 54 us -> 0 us
  other arithmetic: 34 us -> 0 us
  local copies, waits for them, and re-layouts: 42.4 us -> 8.46 us
  starting transfers between devices: 29.3 us -> 0 us
  between operations: 14.2 us -> 0.64 us
    pallas_call x0 -> x1, Pallas kernels: none -> 211 us  [on_device(): pl.pallas_call(kernel, out_shape=(jax.ShapeDtypeStruct((128, 4096), BF),...]
    all_to_all x2 -> x0, blocking collectives: 116 us -> none  [the longest x1 60.5 us: on_device(): lax.all_to_all(grad_send, 'expert', split_axis=0, concat_axis=0, tiled=True)]
    all_to_all x3 -> x0, waiting for transfers between devices: 91.5 us -> none  [the longest x1 47.5 us: on_device(): lax.all_to_all(grad_rows, 'expert', split_axis=0, concat_axis=0, tiled=True)]
    dot_general x7 -> x0, matrix products: 54 us -> none  [the longest x1 10.7 us: on_device(): jnp.einsum('sech,elh->secl', grad_pre, expert_up, preferred_element_type=...]
    psum x1 -> x0, waiting for transfers between devices: 28.8 us -> none  [on_device(): lax.psum(partial_grad.astype(jnp.bfloat16), 'dp').astype(jnp.float32)]
    all_to_all x3 -> x0, starting transfers between devices: 28.4 us -> none  [the longest x1 12.2 us: on_device(): lax.all_to_all(grad_out, 'expert', split_axis=1, concat_axis=0, tiled=True)]
    another operation x3 -> x0, other arithmetic: 18.2 us -> none
    reshape x4 -> x0, local copies, waits for them, and re-layouts: 14.3 us -> none  [the longest x1 3.64 us: on_device(): grad_back.reshape(-1, width)[target].astype(jnp.float32)]
  transfers between devices with their start and end apart: 6 -> 0, of which waited for: 6 -> 0; matrix products, arithmetic and copies ran while one was open for 28% -> 0% of each run, Pallas kernels for 0% -> 0%
where the time goes in v1:
time: 220 us
  Pallas kernels  211 us (96%)
  local copies, waits for them, and re-layouts  8.46 us (4%)
    pallas_call x1, Pallas kernels, on_device(): pl.pallas_call(kernel, out_shape=(jax.ShapeDtypeStruct((128, 4096), BF),...  211 us
    unnamed x5, local copies, waits for them, and re-layouts  8.46 us

profile of v1, /device:TPU:7, one launch (start us, length us, event | category | flops | bytes accessed | tf_op | source)
XLA Modules:
  0.0 220.1 jit_solution(15242930671596786712)
XLA Ops:
  0.6 1.4 copy.10.routes
  2.0 1.4 copy.11.gates
  3.5 211.0 %moe_layer.1 = (bf16[128,4096]{1,0:T(8,128)(2,1)}, bf16[128,1024]{1,0:T(8,128)(2,1)}, f32[64,1024]{1,0:T(8,128)}) custom-call(bf16[128,1024]{1,0:T(8,128)(2,1)} %latent.1, s32[128,8]{1,0:T(8,128)} %copy.10.routes, f32[128,8]{1,0:T(8,128)} %copy.11.gates, bf16[64,1024]{1,0:T(8,128)(2,1)} %w_own.1, bf16[128,4096]{1,0:T(8,128)(2,1)} %grad_out.1, ...), custom_call_target="tpu_custom_call" | custom-call | flops 24999999488 | bytes 20000000 | tf_op jit(solution)/shard_map/moe_layer/pallas_call | solution.py:447
  214.4 2.3 %copy.15 = bf16[128,4096]{1,0:T(8,128)(2,1)} copy(bf16[128,4096]{1,0:T(8,128)(2,1)} %get-tuple-element.6) | data formatting | bytes 2097152
  216.7 1.7 copy.16
  218.4 1.7 copy.17

commit v2 on v0

v2 whole, which is shorter than its diff:
```python
import jax
import jax.numpy as jnp
from jax import lax
from jax.experimental import pallas as pl
from jax.experimental.pallas import tpu as pltpu
from jax.sharding import PartitionSpec as P

BF = jnp.bfloat16
F32 = jnp.float32
I32 = jnp.int32
MESH = pl.DeviceIdType.MESH
STRIDE = 11
CHUNKS = 4
PER = 8
MAIN = 256
EXTRA = 64
ROWS = 320


def iota(shape, dim):
    return lax.broadcasted_iota(I32, shape, dim)


def dot(a, b, ca=1, cb=0):
    return lax.dot_general(a, b, (((ca,), (cb,)), ((), ())), preferred_element_type=F32)


def index_of(y, z, x, c):
    return ((y * 2 + z) * 4 + x) * 2 + c


def rows_at(start, size):
    return pl.ds(pl.multiple_of(start, size), size)


def kernel(
    latent, routes, gates, w_own, grad_out, up_hbm, down_hbm,
    mixed, grad_latent, grad_w,
    s1, r1, b1, s2, r2, b2, up, down, relu, xc, acc, extra,
    routes2, gates2, latent2, gc2, part_f, part_b,
    go, wj, pga, pgb, pgs, pgr, cb, mps, gwp, gwy, gws, gwx, dps, dpr,
    sel, selt, p_send, pg_send, p_back, pg_back,
    a2a_ss, a2a_rs, bud_ss, bud_rs, wx_ss, wx_rs, wy_ss, wy_rs, go_ss, go_rs,
    pga_sem, pg_ss, pg_rs, cb_ss, cb_rs, cf_ss, mx_ss, mx_rs,
    gy_ss, gy_rs, gx_ss, gx_rs, dp_sem, loc,
):
    dp = lax.axis_index("dp")
    me = lax.axis_index("expert")
    y, z, x, c = me // 16, (me // 8) % 2, (me // 2) % 4, me % 2
    ring = dp * 2 + z
    mine = c * 4 + ring
    here = y * 8 + x * 2 + c
    sibling = index_of(y, z, x, 1 - c)
    buddy = index_of(y, 1 - z, x, c)
    half, parity = x // 2, x % 2

    def partner(k, sign):
        off = (STRIDE * k) % 32
        py, px, pc = (y + sign * (off // 8) + 4) % 4, (x + sign * ((off // 2) % 4) + 4) % 4, (c + off) % 2
        return index_of(py, z, px, pc), py * 8 + px * 2 + pc

    def ring_at(d):
        to = (ring + d) % 4
        return to, to // 2, index_of(y, to % 2, x, c)

    def member(dc, dz):
        to, cc = (ring + dz) % 4, (c + dc) % 2
        return cc * 4 + to, to // 2, index_of(y, to % 2, x, cc)

    others = [(dc, dz) for dz in (1, 3, 2, 0) for dc in (0, 1) if dc or dz]

    def remote(src, dst, ss, rs, dev, rep=None):
        rep = dp if rep is None else rep
        return pltpu.make_async_remote_copy(src, dst, ss, rs, device_id=(rep, dev), device_id_type=MESH)

    barrier = pltpu.get_barrier_semaphore()

    def greet(k, carry):
        pl.semaphore_signal(barrier, inc=1, device_id=(dp, partner(k, 1)[0]), device_id_type=MESH)
        return carry

    lax.fori_loop(1, 32, greet, 0)
    for dc, dz in others:
        if dz:
            _, rep, to = member(dc, dz)
            pl.semaphore_signal(barrier, inc=1, device_id=(rep, to), device_id_type=MESH)
    up_copy = pltpu.make_async_copy(up_hbm.at[0], up, loc.at[0])
    down_copy = pltpu.make_async_copy(down_hbm.at[0], down, loc.at[1])
    up_copy.start()
    down_copy.start()
    routes2[z] = routes[...]
    gates2[z] = gates[...]
    latent2[rows_at(z * 128, 128), :] = latent[...]

    i, j = iota((256, 256), 0), iota((256, 256), 1)
    sel[...] = jnp.where(((i & 63) >> 2) * 16 + (i >> 6) * 4 + (i & 3) == j, 1.0, 0.0).astype(BF)
    selt[...] = jnp.where(((j & 63) >> 2) * 16 + (j >> 6) * 4 + (j & 3) == i, 1.0, 0.0).astype(BF)

    pl.semaphore_wait(barrier, 37)

    own_tokens = rows_at(z * 128, 128)
    swap = [
        remote(routes, routes2.at[z], bud_ss.at[0], bud_rs.at[0], buddy),
        remote(gates, gates2.at[z], bud_ss.at[1], bud_rs.at[1], buddy),
        remote(latent, latent2.at[own_tokens], bud_ss.at[2], bud_rs.at[2], buddy),
    ]
    for copy in swap:
        copy.start()

    sends_w = parity == (y + dp) % 2
    w_slot = rows_at(y * 128 + c * 64, 64)

    def wx(d):
        to = index_of(y, z, (x + d) % 4, half)
        return to, remote(w_own, wj.at[w_slot], wx_ss.at[d], wx_rs.at[c], to)

    for d in (1, 3, 2, 0):
        to, copy = wx(d)
        go_on = jnp.logical_and(sends_w, to != me)

        @pl.when(go_on)
        def _():
            copy.start()

        if d == 0:

            @pl.when(jnp.logical_and(sends_w, to == me))
            def _():
                wj[w_slot, :] = w_own[...]

    def feats(m, part):
        to = m % 4
        return rows_at(part * 1024 + (to % 2) * 512 + (m // 4) * 256 + ((part + to // 2) % 2) * 128, 128)

    def tokens(m):
        return rows_at(m * 128, 128)

    own_go = []
    for part in range(4):
        cols = pl.ds(part * 128, 128)
        for n, (dc, dz) in enumerate(others):
            m, rep, to = member(dc, dz)
            remote(grad_out.at[:, feats(m, part)], go.at[tokens(mine), cols], go_ss.at[n], go_rs.at[mine], to, rep).start()
        copy = pltpu.make_async_copy(grad_out.at[:, feats(mine, part)], go.at[tokens(mine), cols], loc.at[2 + part])
        copy.start()
        own_go.append(copy)

    x_own = c * 2 + (y + dp) % 2
    for cc in range(2):
        src = index_of(y, z, x_own, cc)

        @pl.when(src != me)
        def _():
            remote(w_own, wj.at[rows_at(y * 128 + cc * 64, 64)], wx_ss.at[0], wx_rs.at[cc], me).wait_recv()

    def along_y(d):
        py = (y + d) % 4
        return py, index_of(py, z, x, c)

    def wy(d):
        _, to = along_y(d)
        return remote(wj.at[tokens(y)], wj.at[tokens(y)], wy_ss.at[d], wy_rs.at[y], to)

    for d in (1, 3, 2):
        wy(d).start()

    swap[0].wait_recv()
    swap[1].wait_recv()

    def names(j):
        return jnp.where(j < 1024, j >> 4, (j - 1024) >> 2), jnp.where(j < 1024, j & 15, 16 + (j & 3)) + 1

    def expert_of(pair):
        p = pair >> 1
        return (p >> 3) * 16 + z * 8 + (p & 7)

    pair_r, s_row = names(iota((1280, 128), 0))
    pair_c, s_col = names(iota((128, 1280), 1))
    named_r = expert_of(pair_r) == iota((1280, 128), 1)
    named_c = expert_of(pair_c) == iota((128, 1280), 0)
    earlier = jnp.where(iota((128, 128), 0) < iota((128, 128), 1), 1.0, 0.0).astype(BF)
    for zs in range(2):
        rt = routes2[zs]
        gt = gates2[zs]
        expert = iota((128, 128), 0)
        hot = jnp.zeros((128, 128), F32)
        gate = jnp.zeros((128, 128), F32)
        for k in range(8):
            hit = rt[k : k + 1, :] == expert
            hot = hot + jnp.where(hit, 1.0, 0.0)
            gate = gate + jnp.where(hit, gt[k : k + 1, :], 0.0)
        slot = jnp.where(hot > 0.5, dot(hot.astype(BF), earlier) + 1.0, 0.0)
        gate_hi = gate.astype(BF).astype(F32)
        gate_lo = gate - gate_hi
        t0, t1 = zs * 128, zs * 128 + 128
        spread_t = jnp.where(jnp.logical_and(named_r, (pair_r & 1) == zs), 1.0, 0.0).astype(BF)
        hit_t = dot(spread_t, slot.astype(BF)) == s_row.astype(F32)
        p_send[:, t0:t1] = jnp.where(hit_t, 1.0, 0.0).astype(BF)
        pg_send[:, t0:t1] = jnp.where(hit_t, dot(spread_t, gate_hi.astype(BF)), 0.0).astype(BF)
        pg_send[:, 256 + t0 : 256 + t1] = jnp.where(hit_t, dot(spread_t, gate_lo.astype(BF)), 0.0).astype(BF)
        spread = jnp.where(jnp.logical_and(named_c, (pair_c & 1) == zs), 1.0, 0.0).astype(BF)
        hit_b = dot(slot.T.astype(BF), spread) == s_col.astype(F32)
        p_back[t0:t1, :] = jnp.where(hit_b, 1.0, 0.0).astype(BF)
        pg_back[t0:t1, :] = jnp.where(hit_b, dot(gate_hi.T.astype(BF), spread), 0.0).astype(BF)
        pg_back[256 + t0 : 256 + t1, :] = jnp.where(hit_b, dot(gate_lo.T.astype(BF), spread), 0.0).astype(BF)

    def unpack(packed):
        rows = dot(sel[...], packed).astype(BF)
        return jnp.concatenate([rows[q * 64 : (q + 1) * 64] for q in range(4)], axis=1)

    def pack(rows):
        stacked = jnp.concatenate([rows[:, q * 256 : (q + 1) * 256] for q in range(4)], axis=0)
        return dot(selt[...], stacked).astype(BF)

    def main_rows(ci):
        return rows_at(ci * MAIN, MAIN)

    def fill(pick, source, buffer):
        def body(ci, carry):
            buffer[main_rows(ci), 0:1024] = dot(pick[main_rows(ci), :], source[...]).astype(BF)
            more = pick[rows_at(1024 + ci * EXTRA, EXTRA), :]
            buffer[main_rows(ci), 1024:1280] = pack(dot(more, source[...]).astype(BF))
            return carry

        lax.fori_loop(0, CHUNKS, body, 0)

    def block(k):
        return rows_at(k * 32, 32)

    def start_out(which, src, dst):
        def body(k, carry):
            to, p = partner(k, 1)
            remote(src.at[block(p)], dst.at[block(k)], a2a_ss.at[which], a2a_rs.at[which, k // PER], to).start()
            return carry

        lax.fori_loop(1, 32, body, 0)
        dst[0:32, :] = src[block(here), :]

    def start_back(which, src, dst, ci):
        def body(k, carry):
            to, _ = partner(k, -1)
            remote(src.at[block(k)], dst.at[block(here)], a2a_ss.at[which], a2a_rs.at[which, k // PER], to).start()
            return carry

        lax.fori_loop(jnp.maximum(ci * PER, 1), ci * PER + PER, body, 0)

        @pl.when(ci == 0)
        def _():
            dst[block(here), :] = src[0:32, :]

    def arrived(which, ci, src, dst, first):
        rows = pl.ds(0, 224) if first else main_rows(ci)
        remote(src.at[rows], dst.at[rows], a2a_ss.at[which], a2a_rs.at[which, ci], me).wait_recv()

    def all_sent(which, src, dst):
        rows = pl.ds(0, 992)
        remote(src.at[rows], dst.at[rows], a2a_ss.at[which], a2a_rs.at[which, 0], me).wait_send()

    swap[2].wait_recv()
    fill(p_send, latent2, s1)
    start_out(0, s1, r1)

    for d in (1, 3, 2):
        py, _ = along_y(d)
        remote(wj.at[tokens(py)], wj.at[tokens(py)], wy_ss.at[d], wy_rs.at[py], me).wait_recv()
    for copy in own_go:
        copy.wait()
    for n, (dc, dz) in enumerate(others):
        m, _, _ = member(dc, dz)
        remote(go.at[tokens(m)], go.at[tokens(m)], go_ss.at[n], go_rs.at[m], me).wait_recv()

    def quarter(n):
        return rows_at(n * 256, 256)

    def core_rows(cc):
        return rows_at(cc * 512, 512)

    def for_sibling(n, carry):
        pga[:, quarter(n)] = dot(go[core_rows(1 - c), :], wj[:, quarter(n)]).astype(BF)
        return carry

    lax.fori_loop(0, 4, for_sibling, 0)
    to_sibling = remote(pga, pgb, pga_sem.at[0], pga_sem.at[1], sibling)
    to_sibling.start()
    to_sibling.wait_recv()

    def for_own(n, carry):
        pgs[:, quarter(n)] = (dot(go[core_rows(c), :], wj[:, quarter(n)]) + pgb[:, quarter(n)].astype(F32)).astype(BF)
        return carry

    lax.fori_loop(0, 4, for_own, 0)
    for d in (1, 3, 2):
        to, rep, dev = ring_at(d)
        remote(pgs.at[tokens(to)], pgr.at[tokens(ring)], pg_ss.at[d], pg_rs.at[ring], dev, rep).start()
    pgr[tokens(ring), :] = pgs[tokens(ring), :]
    for d in (1, 3, 2):
        to, _, _ = ring_at(d)
        remote(pgs.at[tokens(to)], pgr.at[tokens(to)], pg_ss.at[d], pg_rs.at[to], me).wait_recv()
    gc = sum(pgr[n * 128 : (n + 1) * 128, :].astype(F32) for n in range(4)).astype(BF)
    gc2[own_tokens, :] = gc
    gc2[rows_at(256 + z * 128, 128), :] = gc
    swap_gc = remote(gc2.at[own_tokens], gc2.at[own_tokens], bud_ss.at[3], bud_rs.at[3], buddy)
    swap_gc.start()
    swap_gc.wait_recv()
    gc2[rows_at(256 + (1 - z) * 128, 128), :] = gc2[rows_at((1 - z) * 128, 128), :]
    fill(pg_send, gc2, s2)
    start_out(2, s2, r2)

    up_copy.wait()
    down_copy.wait()

    def load(src, ci):
        xc[0:MAIN, :] = src[main_rows(ci), 0:1024]
        xc[MAIN:ROWS, :] = unpack(src[main_rows(ci), 1024:1280])

    def store(dst, ci):
        dst[main_rows(ci), 0:1024] = acc[0:MAIN, :].astype(BF)
        dst[main_rows(ci), 1024:1280] = pack(acc[MAIN:ROWS, :].astype(BF))

    def hidden(h):
        return rows_at(h * 512, 512)

    def arrived_chunk(which, ci, src, dst):
        @pl.when(ci == 0)
        def _():
            arrived(which, 0, src, dst, True)

        @pl.when(ci > 0)
        def _():
            arrived(which, ci, src, dst, False)

    def forward(ci, carry):
        arrived_chunk(0, ci, s1, r1)
        load(r1, ci)
        acc[...] = jnp.zeros_like(acc)

        def step(h, inner):
            pos = jnp.maximum(dot(xc[...], up[:, hidden(h)]), 0.0)
            relu[ci, :, hidden(h)] = pos
            acc[...] += dot((pos * pos).astype(BF), down[hidden(h), :])
            return inner

        lax.fori_loop(0, 4, step, 0)
        store(r1, ci)
        start_back(1, r1, b1, ci)
        return carry

    lax.fori_loop(0, CHUNKS, forward, 0)

    def backward(ci, carry):
        arrived_chunk(2, ci, s2, r2)
        load(r2, ci)
        acc[...] = jnp.zeros_like(acc)

        def step(h, inner):
            grad = dot(xc[...], down[hidden(h), :], 1, 1) * 2.0 * relu[ci, :, hidden(h)]
            acc[...] += dot(grad.astype(BF), up[:, hidden(h)], 1, 1)
            return inner

        lax.fori_loop(0, 4, step, 0)
        store(r2, ci)
        start_back(3, r2, b2, ci)
        return carry

    lax.fori_loop(0, CHUNKS, backward, 0)

    def gather_back(which, src, dst):
        for ci in range(CHUNKS):
            arrived(which, ci, src, dst, ci == 0)

        def body(ci, carry):
            extra[rows_at(ci * EXTRA, EXTRA), :] = unpack(dst[main_rows(ci), 1024:1280])
            return carry

        lax.fori_loop(0, CHUNKS, body, 0)

    def swap_part(n, slot):
        part_b[slot] = part_f[rows_at((1 - z) * 128, 128), :].astype(BF)
        copy = remote(part_b.at[slot], part_b.at[slot + 1], bud_ss.at[n], bud_rs.at[n], buddy)
        copy.start()
        return copy

    gather_back(1, r1, b1)

    def combine(n, carry):
        cols = quarter(n)
        both = dot(pg_back[:, 0:1024], b1[:, cols])
        both = both + dot(pg_back[:, 1024:1280], extra[:, cols])
        part_f[:, cols] = both[0:256] + both[256:512]
        return carry

    lax.fori_loop(0, 4, combine, 0)
    swap_c = swap_part(4, 0)
    swap_c.wait_recv()
    cb[tokens(mine), :] = (part_f[own_tokens, :] + part_b[1].astype(F32)).astype(BF)

    def cb_copy(m, ss, dev, rep):
        return remote(cb.at[tokens(m)], cb.at[tokens(m)], ss, cb_rs.at[m], dev, rep)

    for d in (1, 3, 2):
        _, rep, dev = ring_at(d)
        cb_copy(mine, cb_ss.at[d], dev, rep).start()
    cb_copy(mine, cb_ss.at[0], sibling, dp).start()
    for d in (1, 3, 2):
        to, _, _ = ring_at(d)
        m = c * 4 + to
        cb_copy(m, cb_ss.at[d], me, dp).wait_recv()
        cb_copy(m, cf_ss.at[d], sibling, dp).start()
    for d in range(4):
        m = (1 - c) * 4 + (ring + d) % 4
        cb_copy(m, cb_ss.at[d], me, dp).wait_recv()

    def gy(d):
        py, to = along_y(d)
        return py, remote(gwp.at[tokens(py)], gwy.at[tokens(y)], gy_ss.at[d], gy_rs.at[y], to)

    def weight_grad(n, carry):
        py = (y + 3 - n) % 4
        gwp[tokens(py), :] = dot(go[:, tokens(py)], cb[...], 0, 0).astype(BF)

        @pl.when(n < 3)
        def _():
            to = index_of(py, z, x, c)
            remote(gwp.at[tokens(py)], gwy.at[tokens(y)], gy_ss.at[3 - n], gy_rs.at[y], to).start()

        return carry

    lax.fori_loop(0, 4, weight_grad, 0)
    gwy[tokens(y), :] = gwp[tokens(y), :]

    def mix(part, carry):
        cols = tokens(part)
        mps[:, cols] = dot(cb[...], wj[cols, :], 1, 1).astype(BF)
        for n, (dc, dz) in enumerate(others):
            m, rep, to = member(dc, dz)
            remote(mps.at[tokens(m), cols], mixed.at[:, feats(mine, part)], mx_ss.at[n], mx_rs.at[mine], to, rep).start()
        mixed[:, feats(mine, part)] = mps[tokens(mine), cols]
        return carry

    lax.fori_loop(0, 4, mix, 0)

    for d in (1, 3, 2):
        py, _ = along_y(d)
        remote(gwp.at[tokens(py)], gwy.at[tokens(py)], gy_ss.at[d], gy_rs.at[py], me).wait_recv()
    gws[...] = sum(gwy[n * 128 : (n + 1) * 128, :].astype(F32) for n in range(4)).astype(BF)
    x_slot = rows_at(x * 64, 64)

    def gx(cc):
        to = index_of(y, z, x_own, cc)
        return to, remote(gws.at[pl.ds(cc * 64, 64)], gwx.at[x_slot], gx_ss.at[cc], gx_rs.at[x], to)

    for cc in range(2):
        to, copy = gx(cc)

        @pl.when(to != me)
        def _():
            copy.start()

        @pl.when(to == me)
        def _():
            gwx[x_slot, :] = gws[cc * 64 : cc * 64 + 64, :]

    exchange = pltpu.make_async_remote_copy(
        dps, dpr, dp_sem.at[0], dp_sem.at[1], device_id=(1 - dp, me), device_id_type=MESH
    )

    @pl.when(sends_w)
    def _():
        for px in range(4):
            src = index_of(y, z, px, half)

            @pl.when(src != me)
            def _():
                rows = pl.ds(px * 64, 64)
                remote(gwx.at[rows], gwx.at[rows], gx_ss.at[0], gx_rs.at[px], me).wait_recv()

        dps[...] = sum(gwx[n * 64 : (n + 1) * 64, :].astype(F32) for n in range(4)).astype(BF)
        exchange.start()

    gather_back(3, r2, b2)

    def combine_back(n, carry):
        cols = quarter(n)
        part_f[:, cols] = dot(p_back[:, 0:1024], b2[:, cols]) + dot(p_back[:, 1024:1280], extra[:, cols])
        return carry

    lax.fori_loop(0, 4, combine_back, 0)
    swap_g = swap_part(5, 2)
    swap_g.wait_recv()
    grad_latent[...] = (part_f[own_tokens, :] + part_b[3].astype(F32)).astype(BF)

    @pl.when(sends_w)
    def _():
        exchange.wait_send()
        grad_w[...] = dps[...].astype(F32)

    @pl.when(jnp.logical_not(sends_w))
    def _():
        exchange.wait_recv()
        grad_w[...] = dpr[...].astype(F32)

    for n, (dc, dz) in enumerate(others):
        m, _, _ = member(dc, dz)
        whole = remote(mps.at[tokens(m)], mps.at[tokens(m)], mx_ss.at[n], mx_rs.at[m], me)
        whole.wait_recv()
        whole.wait_send()
        remote(go.at[tokens(m)], go.at[tokens(m)], go_ss.at[n], go_rs.at[m], me).wait_send()
    for copy in swap + [swap_gc, swap_c, swap_g, to_sibling]:
        copy.wait_send()
    for d in range(4):
        to, copy = wx(d)
        go_on = jnp.logical_and(sends_w, to != me)

        @pl.when(go_on)
        def _():
            copy.wait_send()

        cb_copy(mine, cb_ss.at[d], me, dp).wait_send()
        if d:
            wy(d).wait_send()
            gy(d)[1].wait_send()
            cb_copy(mine, cf_ss.at[d], me, dp).wait_send()
            remote(pgs.at[tokens(0)], pgr.at[tokens(0)], pg_ss.at[d], pg_rs.at[0], me).wait_send()
    for cc in range(2):
        to, copy = gx(cc)

        @pl.when(to != me)
        def _():
            copy.wait_send()

    all_sent(0, s1, r1)
    all_sent(1, r1, b1)
    all_sent(2, s2, r2)
    all_sent(3, r2, b2)


def on_device(latent, routes, gates, grad_out, w_out_t, expert_up, expert_down):
    vm = pl.BlockSpec(memory_space=pltpu.VMEM)
    hbm = pl.BlockSpec(memory_space=pl.ANY)

    def dma(*shape):
        return pltpu.SemaphoreType.DMA(shape)

    def bf(*shape):
        return pltpu.VMEM(shape, BF)

    scratch = [bf(1024, 1280)] * 6 + [
        bf(1024, 2048), bf(2048, 1024), pltpu.VMEM((CHUNKS, ROWS, 2048), F32),
        bf(ROWS, 1024), pltpu.VMEM((ROWS, 1024), F32), bf(256, 1024),
        pltpu.VMEM((2, 8, 128), I32), pltpu.VMEM((2, 8, 128), F32), bf(256, 1024), bf(512, 1024),
        pltpu.VMEM((256, 1024), F32), bf(4, 128, 1024),
        bf(1024, 512), bf(512, 1024), bf(512, 1024), bf(512, 1024), bf(512, 1024), bf(512, 1024),
        bf(1024, 1024), bf(1024, 512), bf(512, 1024), bf(512, 1024), bf(128, 1024), bf(256, 1024),
        bf(64, 1024), bf(64, 1024),
        bf(256, 256), bf(256, 256), bf(1280, 256), bf(1280, 512), bf(256, 1280), bf(512, 1280),
        dma(4), dma(4, 4), dma(6), dma(6), dma(4), dma(2), dma(4), dma(4), dma(7), dma(8),
        dma(2), dma(4), dma(4), dma(4), dma(8), dma(4), dma(7), dma(8),
        dma(4), dma(4), dma(2), dma(4), dma(2), dma(6),
    ]
    return pl.pallas_call(
        kernel,
        out_shape=(
            jax.ShapeDtypeStruct((128, 4096), BF),
            jax.ShapeDtypeStruct((128, 1024), BF),
            jax.ShapeDtypeStruct((64, 1024), F32),
        ),
        in_specs=[vm, vm, vm, vm, hbm, hbm, hbm],
        out_specs=(vm, vm, vm),
        scratch_shapes=scratch,
        compiler_params=pltpu.CompilerParams(
            collective_id=0, has_side_effects=True, vmem_limit_bytes=63 * 1024 * 1024
        ),
        cost_estimate=pl.CostEstimate(flops=25_000_000_000, bytes_accessed=20_000_000, transcendentals=0),
        name="moe_layer",
    )(latent, routes.T, gates.T, w_out_t, grad_out, expert_up, expert_down)


def solution(mesh):
    rows = P(("dp", "expert"), None)
    return jax.shard_map(
        on_device,
        mesh=mesh,
        in_specs=(rows, rows, rows, rows, P("expert", None), P("expert", None, None), P("expert", None, None)),
        out_specs=(rows, rows, P("expert", None)),
        check_vma=False,
    )
```

time: 431 us -> 213 us (0.49)
  the two profiles are of different devices: /device:TPU:7 before, /device:TPU:43 now
where the time goes in v2:
time: 213 us
  Pallas kernels  207 us (97%)
  local copies, waits for them, and re-layouts  5.63 us (3%)
    pallas_call x1, Pallas kernels, on_device(): pl.pallas_call(kernel, out_shape=(jax.ShapeDtypeStruct((128, 4096), BF),...  207 us
    unnamed x3, local copies, waits for them, and re-layouts  5.63 us

profile of v2, /device:TPU:43, one launch (start us, length us, event | category | flops | bytes accessed | tf_op | source)
XLA Modules:
  0.0 213.2 jit_solution(15881326395113686157)
XLA Ops:
  0.6 206.9 %moe_layer.1 = (bf16[128,4096]{1,0:T(8,128)(2,1)}, bf16[128,1024]{1,0:T(8,128)(2,1)}, f32[64,1024]{1,0:T(8,128)}) custom-call(bf16[128,1024]{1,0:T(8,128)(2,1)} %latent.1, s32[8,128]{1,0:T(8,128)} %bitcast.2, f32[8,128]{1,0:T(8,128)} %bitcast.3, bf16[64,1024]{1,0:T(8,128)(2,1)} %w_own.1, bf16[128,4096]{1,0:T(8,128)(2,1)} %grad_out.1, ...), custom_call_target="tpu_custom_call" | custom-call | flops 24999999488 | bytes 20000000 | tf_op jit(solution)/shard_map/moe_layer/pallas_call | solution.py:560
  207.6 2.3 %copy.13 = bf16[128,4096]{1,0:T(8,128)(2,1)} copy(bf16[128,4096]{1,0:T(8,128)(2,1)} %get-tuple-element.6) | data formatting | bytes 2097152
  209.8 1.7 copy.14
  211.5 1.7 copy.15

commit v3 on v2

v3 whole, which is shorter than its diff:
```python
import jax
import jax.numpy as jnp
from jax import lax
from jax.experimental import pallas as pl
from jax.experimental.pallas import tpu as pltpu
from jax.sharding import PartitionSpec as P

BF = jnp.bfloat16
F32 = jnp.float32
I32 = jnp.int32
MESH = pl.DeviceIdType.MESH
STRIDE = 5
CHUNKS = 4
PER = 4
MAIN = 256
EXTRA = 64
ROWS = 320


def iota(shape, dim):
    return lax.broadcasted_iota(I32, shape, dim)


def dot(a, b, ca=1, cb=0):
    return lax.dot_general(a, b, (((ca,), (cb,)), ((), ())), preferred_element_type=F32)


def index_of(y, z, x, c):
    return ((y * 2 + z) * 4 + x) * 2 + c


def rows_at(start, size):
    return pl.ds(pl.multiple_of(start, size), size)


def kernel(
    latent, routes, gates, w_own, grad_out, up_hbm, down_hbm,
    mixed, grad_latent, grad_w,
    s1, r1, b1, s2, r2, b2, up, down, relu, xc, acc, extra,
    routes4, gates4, latent4, gc4, part_f, part_s, part_r,
    go, wj, pga, pgb, pgs, pgr, cb, mps, gwp, gwy, gws, gwx, dps, dpr,
    slots, gate_tab, sel, selt, p_send, pg_send, p_back, pg_back,
    a2a_ss, a2a_rs, grp_ss, grp_rs, sw_ss, sw_rs, wx_ss, wx_rs, wy_ss, wy_rs, go_ss, go_rs,
    sib_ss, sib_rs, bgc_ss, bgc_rs, pg_ss, pg_rs, cb_ss, cb_rs, cf_ss, mx_ss, mx_rs,
    gy_ss, gy_rs, gx_ss, gx_rs, dp_sem, loc,
):
    dp = lax.axis_index("dp")
    me = lax.axis_index("expert")
    y, z, x, c = me // 16, (me // 8) % 2, (me // 2) % 4, me % 2
    ring = dp * 2 + z
    mine = c * 4 + ring
    sibling = index_of(y, z, x, 1 - c)
    block = x * (1 - c) + y * c
    half, parity = x // 2, x % 2

    def partner(k, sign):
        off = (STRIDE * k) % 16
        along, hop, flip = off // 4, (off // 2) % 2, off % 2
        pc = (c + flip) % 2
        sender, expert = (c, pc) if sign > 0 else (pc, c)
        pr = (ring + sign * hop * (1 - 2 * expert) + 4) % 4
        py, px = (y + sign * along * (1 - sender) + 4) % 4, (x + sign * along * sender + 4) % 4
        return pr // 2, index_of(py, pr % 2, px, pc)

    def group_at(d):
        to = (block + d) % 4
        return to, index_of(y + c * (to - y), z, x + (1 - c) * (to - x), c)

    def ring_at(d):
        to = (ring + d) % 4
        return to, to // 2, index_of(y, to % 2, x, c)

    def member(dc, dz):
        to, cc = (ring + dz) % 4, (c + dc) % 2
        return cc * 4 + to, to // 2, index_of(y, to % 2, x, cc)

    others = [(dc, dz) for dz in (1, 3, 2, 0) for dc in (0, 1) if dc or dz]

    def remote(src, dst, ss, rs, dev, rep=None):
        rep = dp if rep is None else rep
        return pltpu.make_async_remote_copy(src, dst, ss, rs, device_id=(rep, dev), device_id_type=MESH)

    barrier = pltpu.get_barrier_semaphore()

    def signal(rep, dev):
        pl.semaphore_signal(barrier, inc=1, device_id=(rep, dev), device_id_type=MESH)

    def greet(k, carry):
        for sign in (1, -1):
            signal(*partner(k, sign))
        return carry

    lax.fori_loop(1, 16, greet, 0)
    for dc, dz in others:
        _, rep, to = member(dc, dz)
        signal(rep, to)
    for d in range(1, 8):
        near = (x * 2 + c + d) % 8
        signal(dp, index_of(y, z, near // 2, near % 2))
    for d in range(1, 4):
        signal(dp, index_of((y + d) % 4, z, x, c))
    up_copy = pltpu.make_async_copy(up_hbm.at[0], up, loc.at[0])
    down_copy = pltpu.make_async_copy(down_hbm.at[0], down, loc.at[1])
    up_copy.start()
    down_copy.start()
    own_tokens = rows_at(block * 128, 128)
    routes4[block] = routes[...]
    gates4[block] = gates[...]
    latent4[own_tokens, :] = latent[...]

    i, j = iota((256, 256), 0), iota((256, 256), 1)
    sel[...] = jnp.where(((i & 63) >> 2) * 16 + (i >> 6) * 4 + (i & 3) == j, 1.0, 0.0).astype(BF)
    selt[...] = jnp.where(((j & 63) >> 2) * 16 + (j >> 6) * 4 + (j & 3) == i, 1.0, 0.0).astype(BF)

    pl.semaphore_wait(barrier, 47)

    swap = []
    for d in (1, 3, 2):
        _, to = group_at(d)
        swap.append(remote(routes, routes4.at[block], grp_ss.at[0, d], grp_rs.at[0, block], to))
        swap.append(remote(gates, gates4.at[block], grp_ss.at[1, d], grp_rs.at[1, block], to))
    for d in (1, 3, 2):
        _, to = group_at(d)
        swap.append(remote(latent, latent4.at[own_tokens], grp_ss.at[2, d], grp_rs.at[2, block], to))
    for copy in swap:
        copy.start()

    def from_group(n, dst):
        for d in (1, 3, 2):
            g, _ = group_at(d)
            remote(dst(g), dst(g), grp_ss.at[n, d], grp_rs.at[n, g], me).wait_recv()

    sends_w = parity == (y + dp) % 2
    w_slot = rows_at(y * 128 + c * 64, 64)

    def wx(d):
        to = index_of(y, z, (x + d) % 4, half)
        return to, remote(w_own, wj.at[w_slot], wx_ss.at[d], wx_rs.at[c], to)

    for d in (1, 3, 2, 0):
        to, copy = wx(d)
        go_on = jnp.logical_and(sends_w, to != me)

        @pl.when(go_on)
        def _():
            copy.start()

        if d == 0:

            @pl.when(jnp.logical_and(sends_w, to == me))
            def _():
                wj[w_slot, :] = w_own[...]

    def feats(m, part):
        to = m % 4
        return rows_at(part * 1024 + (to % 2) * 512 + (m // 4) * 256 + ((part + to // 2) % 2) * 128, 128)

    def tokens(m):
        return rows_at(m * 128, 128)

    own_go = []
    for part in range(4):
        cols = pl.ds(part * 128, 128)
        for n, (dc, dz) in enumerate(others):
            m, rep, to = member(dc, dz)
            remote(grad_out.at[:, feats(m, part)], go.at[tokens(mine), cols], go_ss.at[n], go_rs.at[mine], to, rep).start()
        copy = pltpu.make_async_copy(grad_out.at[:, feats(mine, part)], go.at[tokens(mine), cols], loc.at[2 + part])
        copy.start()
        own_go.append(copy)

    from_group(0, lambda g: routes4.at[g])
    from_group(1, lambda g: gates4.at[g])

    def names(j):
        return jnp.where(j < 256, j >> 4, (j - 256) >> 2), jnp.where(j < 256, j & 15, 16 + (j & 3)) + 1

    def expert_of(k):
        off = (STRIDE * k) & 15
        along, hop, pc = off >> 2, (off >> 1) & 1, (c + off) & 1
        py, px = (y + along * (1 - c)) & 3, (x + along * c) & 3
        return ((py * 2 + ((z + hop) & 1)) * 4 + px) * 2 + pc

    k_row, s_row = names(iota((320, 128), 0))
    k_col, s_col = names(iota((128, 320), 1))
    spread_t = jnp.where(expert_of(k_row) == iota((320, 128), 1), 1.0, 0.0).astype(BF)
    spread = jnp.where(expert_of(k_col) == iota((128, 320), 0), 1.0, 0.0).astype(BF)
    earlier = jnp.where(iota((128, 128), 0) < iota((128, 128), 1), 1.0, 0.0).astype(BF)

    def table(g):
        hot = jnp.zeros((128, 128), F32)
        gate = jnp.zeros((128, 128), F32)
        for k in range(8):
            hit = routes4[g, k : k + 1, :] == iota((128, 128), 0)
            hot = hot + jnp.where(hit, 1.0, 0.0)
            gate = gate + jnp.where(hit, gates4[g, k : k + 1, :], 0.0)
        slot = jnp.where(hot > 0.5, dot(hot.astype(BF), earlier) + 1.0, 0.0)
        return slot, gate

    for g in range(4):
        slots[g], gate_tab[g] = table(g)
        hit = dot(spread_t, slots[g].astype(BF)) == s_row.astype(F32)
        p_send[g] = jnp.where(hit, 1.0, 0.0).astype(BF)

    def routing_rest():
        for g in range(4):
            gate_hi = gate_tab[g].astype(BF).astype(F32)
            gate_lo = gate_tab[g] - gate_hi
            hit = p_send[g].astype(F32) > 0.5
            pg_send[g, :, 0:128] = jnp.where(hit, dot(spread_t, gate_hi.astype(BF)), 0.0).astype(BF)
            pg_send[g, :, 128:256] = jnp.where(hit, dot(spread_t, gate_lo.astype(BF)), 0.0).astype(BF)
            hit = dot(slots[g].T.astype(BF), spread) == s_col.astype(F32)
            p_back[g] = jnp.where(hit, 1.0, 0.0).astype(BF)
            pg_back[g, 0:128, :] = jnp.where(hit, dot(gate_hi.T.astype(BF), spread), 0.0).astype(BF)
            pg_back[g, 128:256, :] = jnp.where(hit, dot(gate_lo.T.astype(BF), spread), 0.0).astype(BF)

    def unpack(packed):
        rows = dot(sel[...], packed).astype(BF)
        return jnp.concatenate([rows[q * 64 : (q + 1) * 64] for q in range(4)], axis=1)

    def pack(rows):
        stacked = jnp.concatenate([rows[:, q * 256 : (q + 1) * 256] for q in range(4)], axis=0)
        return dot(selt[...], stacked).astype(BF)

    def message(k):
        return rows_at(k * 16, 16)

    def start(which, src, dst, ci, sign):
        def body(k, carry):
            rep, to = partner(k, sign)
            piece = (slice(None), message(k))
            remote(src.at[piece], dst.at[piece], a2a_ss.at[which], a2a_rs.at[which, ci], to, rep).start()
            return carry

        lax.fori_loop(max(ci * PER, 1), ci * PER + PER, body, 0)
        if ci == 0:
            dst[:, 0:16, :] = src[:, 0:16, :]

    def dispatch(which, pick, source, src, dst):
        for g in range(4):
            values = source[g * 128 : g * 128 + 128, :]
            if pick.shape[2] == 256:
                values = jnp.concatenate([values, values], axis=0)
            src[g, :, 0:1024] = dot(pick[g, 0:256, :], values).astype(BF)
            src[g, :, 1024:1280] = pack(dot(pick[g, 256:320, :], values).astype(BF))
        for ci in range(CHUNKS):
            start(which, src, dst, ci, 1)

    def arrived(which, ci, src, dst):
        rows = (slice(None), pl.ds(0, 48) if ci == 0 else pl.ds(ci * 64, 64))
        remote(src.at[rows], dst.at[rows], a2a_ss.at[which], a2a_rs.at[which, ci], me).wait_recv()

    def all_sent(which, src, dst):
        rows = (slice(None), pl.ds(0, 240))
        remote(src.at[rows], dst.at[rows], a2a_ss.at[which], a2a_rs.at[which, 0], me).wait_send()

    x_own = c * 2 + (y + dp) % 2
    for cc in range(2):
        src = index_of(y, z, x_own, cc)

        @pl.when(src != me)
        def _():
            remote(w_own, wj.at[rows_at(y * 128 + cc * 64, 64)], wx_ss.at[0], wx_rs.at[cc], me).wait_recv()

    def along_y(d):
        py = (y + d) % 4
        return py, index_of(py, z, x, c)

    def wy(d):
        _, to = along_y(d)
        return remote(wj.at[tokens(y)], wj.at[tokens(y)], wy_ss.at[d], wy_rs.at[y], to)

    for d in (1, 3, 2):
        wy(d).start()

    from_group(2, lambda g: latent4.at[rows_at(g * 128, 128)])
    dispatch(0, p_send, latent4, s1, r1)
    routing_rest()

    def quarter(n):
        return rows_at(n * 256, 256)

    def core_rows(cc):
        return rows_at(cc * 512, 512)

    def cols_of(q):
        return pl.ds(q * 256, 256)

    to_sibling = []
    swap_gc = []
    for q in range(4):
        cols = cols_of(q)
        to_sibling.append(remote(pga.at[:, cols], pgb.at[:, cols], sib_ss.at[q], sib_rs.at[q], sibling))
        for d in (1, 3, 2):
            piece = gc4.at[own_tokens, cols]
            swap_gc.append(remote(piece, piece, bgc_ss.at[d, q], bgc_rs.at[block, q], group_at(d)[1]))

    def load(src, ci):
        rows = pl.ds(ci * 64, 64)
        for g in range(4):
            xc[g * 64 : g * 64 + 64, :] = src[g, rows, 0:1024]
        xc[MAIN:ROWS, :] = unpack(jnp.concatenate([src[g, rows, 1024:1280] for g in range(4)], axis=0))

    def store(dst, ci):
        rows = pl.ds(ci * 64, 64)
        more = pack(acc[MAIN:ROWS, :].astype(BF))
        for g in range(4):
            dst[g, rows, 0:1024] = acc[g * 64 : g * 64 + 64, :].astype(BF)
            dst[g, rows, 1024:1280] = more[g * 64 : g * 64 + 64, :]

    def hidden(h):
        return rows_at(h * 512, 512)

    def forward(ci):
        arrived(0, ci, s1, r1)
        load(r1, ci)
        acc[...] = jnp.zeros_like(acc)

        def step(h, inner):
            pos = jnp.maximum(dot(xc[...], up[:, hidden(h)]), 0.0)
            relu[ci, :, hidden(h)] = pos
            acc[...] += dot((pos * pos).astype(BF), down[hidden(h), :])
            return inner

        lax.fori_loop(0, 4, step, 0)
        store(r1, ci)
        start(1, r1, b1, ci, -1)

    def backward(ci):
        arrived(2, ci, s2, r2)
        load(r2, ci)
        acc[...] = jnp.zeros_like(acc)

        def step(h, inner):
            grad = dot(xc[...], down[hidden(h), :], 1, 1) * 2.0 * relu[ci, :, hidden(h)]
            acc[...] += dot(grad.astype(BF), up[:, hidden(h)], 1, 1)
            return inner

        lax.fori_loop(0, 4, step, 0)
        store(r2, ci)
        start(3, r2, b2, ci, -1)

    def gc_sibling():
        for d in (1, 3, 2):
            py, _ = along_y(d)
            remote(wj.at[tokens(py)], wj.at[tokens(py)], wy_ss.at[d], wy_rs.at[py], me).wait_recv()
        for copy in own_go:
            copy.wait()
        for n, (dc, dz) in enumerate(others):
            m, _, _ = member(dc, dz)
            remote(go.at[tokens(m)], go.at[tokens(m)], go_ss.at[n], go_rs.at[m], me).wait_recv()
        for q in range(4):
            pga[:, cols_of(q)] = dot(go[core_rows(1 - c), :], wj[:, cols_of(q)]).astype(BF)
            to_sibling[q].start()

    def pg_copy(d, q):
        to, rep, dev = ring_at(d)
        cols = cols_of(q)
        src, dst = pgs.at[tokens(to), cols], pgr.at[tokens(ring), cols]
        return remote(src, dst, pg_ss.at[d, q], pg_rs.at[ring, q], dev, rep)

    def gc_ring():
        for q in range(4):
            cols = cols_of(q)
            to_sibling[q].wait_recv()
            pgs[:, cols] = (dot(go[core_rows(c), :], wj[:, cols]) + pgb[:, cols].astype(F32)).astype(BF)
            for d in (1, 3, 2):
                pg_copy(d, q).start()
            pgr[tokens(ring), cols] = pgs[tokens(ring), cols]

    def gc_swap():
        for q in range(4):
            cols = cols_of(q)
            for d in (1, 3, 2):
                to, _, _ = ring_at(d)
                piece = pgr.at[tokens(to), cols]
                remote(piece, piece, pg_ss.at[d, q], pg_rs.at[to, q], me).wait_recv()
            gc = sum(pgr[n * 128 : (n + 1) * 128, cols].astype(F32) for n in range(4)).astype(BF)
            gc4[own_tokens, cols] = gc
            for n in range(3):
                swap_gc[q * 3 + n].start()

    def gc_dispatch():
        for q in range(4):
            for d in (1, 3, 2):
                g, _ = group_at(d)
                piece = gc4.at[rows_at(g * 128, 128), cols_of(q)]
                remote(piece, piece, bgc_ss.at[d, q], bgc_rs.at[g, q], me).wait_recv()
        dispatch(2, pg_send, gc4, s2, r2)

    def gather_back(which, src, dst):
        for ci in range(CHUNKS):
            arrived(which, ci, src, dst)

        for g in range(4):
            extra[g * EXTRA : g * EXTRA + EXTRA, :] = unpack(dst[g, :, 1024:1280])

    def part_copy(n, d, q):
        g, to = group_at(d)
        cols = cols_of(q)
        src, dst = part_s.at[n, g, :, cols], part_r.at[n, block, :, cols]
        return remote(src, dst, sw_ss.at[n, d, q], sw_rs.at[n, block, q], to)

    def part_sums(n, weights, src):
        for q in range(4):
            cols = cols_of(q)
            for g in range(4):
                both = dot(weights[g, :, 0:256], src[g, :, cols])
                both = both + dot(weights[g, :, 256:320], extra[g * EXTRA : g * EXTRA + EXTRA, cols])
                if weights.shape[1] == 256:
                    both = both[0:128] + both[128:256]
                part_f[g * 128 : g * 128 + 128, cols] = both
                part_s[n, g, :, cols] = both.astype(BF)
            for d in (1, 3, 2):
                part_copy(n, d, q).start()

    def part_total(n, q):
        cols = cols_of(q)
        total = part_f[own_tokens, cols]
        for d in (1, 3, 2):
            g, _ = group_at(d)
            piece = part_r.at[n, g, :, cols]
            remote(piece, piece, sw_ss.at[n, d, q], sw_rs.at[n, g, q], me).wait_recv()
        for d in (1, 3, 2):
            g, _ = group_at(d)
            total = total + part_r[n, g, :, cols].astype(F32)
        return total.astype(BF)

    def combine():
        gather_back(1, r1, b1)
        part_sums(0, pg_back, b1)

    def cb_copy(m, q, ss, dev, rep):
        piece = cb.at[tokens(m), cols_of(q)]
        return remote(piece, piece, ss, cb_rs.at[m, q], dev, rep)

    def share_start():
        for q in range(4):
            cb[tokens(mine), cols_of(q)] = part_total(0, q)
            for d in (1, 3, 2):
                _, rep, dev = ring_at(d)
                cb_copy(mine, q, cb_ss.at[d, q], dev, rep).start()
            cb_copy(mine, q, cb_ss.at[0, q], sibling, dp).start()

    def share_pass():
        for q in range(4):
            for d in (1, 3, 2):
                m = c * 4 + (ring + d) % 4
                cb_copy(m, q, cb_ss.at[d, q], me, dp).wait_recv()
                cb_copy(m, q, cf_ss.at[d, q], sibling, dp).start()

    def gy(d, q):
        py, to = along_y(d)
        cols = cols_of(q)
        src, dst = gwp.at[tokens(py), cols], gwy.at[tokens(y), cols]
        return py, remote(src, dst, gy_ss.at[d, q], gy_rs.at[y, q], to)

    def weight_grad():
        for q in range(4):
            for d in range(4):
                m = (1 - c) * 4 + (ring + d) % 4
                cb_copy(m, q, cb_ss.at[d, q], me, dp).wait_recv()
            cols = cols_of(q)
            gwp[:, cols] = dot(go[...], cb[:, cols], 0, 0).astype(BF)
            for d in (1, 3, 2):
                gy(d, q)[1].start()
            gwy[tokens(y), cols] = gwp[tokens(y), cols]

    def mix_all():
        def mix(part, carry):
            cols = tokens(part)
            mps[:, cols] = dot(cb[...], wj[cols, :], 1, 1).astype(BF)
            for n, (dc, dz) in enumerate(others):
                m, rep, to = member(dc, dz)
                src, dst = mps.at[tokens(m), cols], mixed.at[:, feats(mine, part)]
                remote(src, dst, mx_ss.at[n], mx_rs.at[mine], to, rep).start()
            mixed[:, feats(mine, part)] = mps[tokens(mine), cols]
            return carry

        lax.fori_loop(0, 4, mix, 0)

    up_copy.wait()
    down_copy.wait()
    gc_sibling()
    gc_ring()
    forward(0)
    gc_swap()
    forward(1)
    gc_dispatch()
    forward(2)
    forward(3)
    backward(0)
    backward(1)
    combine()
    backward(2)
    share_start()
    backward(3)
    share_pass()
    weight_grad()
    mix_all()

    for q in range(4):
        for d in (1, 3, 2):
            py, _ = along_y(d)
            piece = gwy.at[tokens(py), cols_of(q)]
            remote(piece, piece, gy_ss.at[d, q], gy_rs.at[py, q], me).wait_recv()
    gws[...] = sum(gwy[n * 128 : (n + 1) * 128, :].astype(F32) for n in range(4)).astype(BF)
    x_slot = rows_at(x * 64, 64)

    def gx(cc):
        to = index_of(y, z, x_own, cc)
        return to, remote(gws.at[pl.ds(cc * 64, 64)], gwx.at[x_slot], gx_ss.at[cc], gx_rs.at[x], to)

    for cc in range(2):
        to, copy = gx(cc)

        @pl.when(to != me)
        def _():
            copy.start()

        @pl.when(to == me)
        def _():
            gwx[x_slot, :] = gws[cc * 64 : cc * 64 + 64, :]

    gather_back(3, r2, b2)
    part_sums(1, p_back, b2)

    exchange = pltpu.make_async_remote_copy(
        dps, dpr, dp_sem.at[0], dp_sem.at[1], device_id=(1 - dp, me), device_id_type=MESH
    )

    @pl.when(sends_w)
    def _():
        for px in range(4):
            src = index_of(y, z, px, half)

            @pl.when(src != me)
            def _():
                rows = pl.ds(px * 64, 64)
                remote(gwx.at[rows], gwx.at[rows], gx_ss.at[0], gx_rs.at[px], me).wait_recv()

        dps[...] = sum(gwx[n * 64 : (n + 1) * 64, :].astype(F32) for n in range(4)).astype(BF)
        exchange.start()
        grad_w[...] = dps[...].astype(F32)

    for q in range(4):
        grad_latent[:, cols_of(q)] = part_total(1, q)

    @pl.when(sends_w)
    def _():
        exchange.wait_send()

    @pl.when(jnp.logical_not(sends_w))
    def _():
        exchange.wait_recv()
        grad_w[...] = dpr[...].astype(F32)

    for n, (dc, dz) in enumerate(others):
        m, _, _ = member(dc, dz)
        whole = remote(mps.at[tokens(m)], mps.at[tokens(m)], mx_ss.at[n], mx_rs.at[m], me)
        whole.wait_recv()
        whole.wait_send()
        remote(go.at[tokens(m)], go.at[tokens(m)], go_ss.at[n], go_rs.at[m], me).wait_send()
    for copy in swap + swap_gc + to_sibling:
        copy.wait_send()
    for d in range(4):
        to, copy = wx(d)
        go_on = jnp.logical_and(sends_w, to != me)

        @pl.when(go_on)
        def _():
            copy.wait_send()

        for q in range(4):
            cb_copy(mine, q, cb_ss.at[d, q], me, dp).wait_send()
            if d:
                gy(d, q)[1].wait_send()
                cb_copy(mine, q, cf_ss.at[d, q], me, dp).wait_send()
        if d:
            wy(d).wait_send()
            for q in range(4):
                pg_copy(d, q).wait_send()
                part_copy(0, d, q).wait_send()
                part_copy(1, d, q).wait_send()
    for cc in range(2):
        to, copy = gx(cc)

        @pl.when(to != me)
        def _():
            copy.wait_send()

    all_sent(0, s1, r1)
    all_sent(1, r1, b1)
    all_sent(2, s2, r2)
    all_sent(3, r2, b2)


def on_device(latent, routes, gates, grad_out, w_out_t, expert_up, expert_down):
    vm = pl.BlockSpec(memory_space=pltpu.VMEM)
    hbm = pl.BlockSpec(memory_space=pl.ANY)

    def dma(*shape):
        return pltpu.SemaphoreType.DMA(shape)

    def bf(*shape):
        return pltpu.VMEM(shape, BF)

    scratch = [bf(4, 256, 1280)] * 6 + [
        bf(1024, 2048), bf(2048, 1024), pltpu.VMEM((CHUNKS, ROWS, 2048), F32),
        bf(ROWS, 1024), pltpu.VMEM((ROWS, 1024), F32), bf(256, 1024),
        pltpu.VMEM((4, 8, 128), I32), pltpu.VMEM((4, 8, 128), F32), bf(512, 1024), bf(512, 1024),
        pltpu.VMEM((512, 1024), F32), bf(2, 4, 128, 1024), bf(2, 4, 128, 1024),
        bf(1024, 512), bf(512, 1024), bf(512, 1024), bf(512, 1024), bf(512, 1024), bf(512, 1024),
        bf(1024, 1024), bf(1024, 512), bf(512, 1024), bf(512, 1024), bf(128, 1024), bf(256, 1024),
        bf(64, 1024), bf(64, 1024),
        pltpu.VMEM((4, 128, 128), F32), pltpu.VMEM((4, 128, 128), F32), bf(256, 256), bf(256, 256),
        bf(4, 320, 128), bf(4, 320, 256), bf(4, 128, 320), bf(4, 256, 320),
        dma(4), dma(4, 4), dma(3, 4), dma(3, 4), dma(2, 4, 4), dma(2, 4, 4), dma(4), dma(2), dma(4), dma(4), dma(7), dma(8),
        dma(4), dma(4), dma(4, 4), dma(4, 4), dma(4, 4), dma(4, 4), dma(4, 4), dma(8, 4), dma(4, 4), dma(7), dma(8),
        dma(4, 4), dma(4, 4), dma(2), dma(4), dma(2), dma(6),
    ]
    return pl.pallas_call(
        kernel,
        out_shape=(
            jax.ShapeDtypeStruct((128, 4096), BF),
            jax.ShapeDtypeStruct((128, 1024), BF),
            jax.ShapeDtypeStruct((64, 1024), F32),
        ),
        in_specs=[vm, vm, vm, vm, hbm, hbm, hbm],
        out_specs=(vm, vm, vm),
        scratch_shapes=scratch,
        compiler_params=pltpu.CompilerParams(
            collective_id=0, has_side_effects=True, vmem_limit_bytes=63 * 1024 * 1024
        ),
        cost_estimate=pl.CostEstimate(flops=25_000_000_000, bytes_accessed=20_000_000, transcendentals=0),
        name="moe_layer",
    )(latent, routes.T, gates.T, w_out_t, grad_out, expert_up, expert_down)


def solution(mesh):
    rows = P(("dp", "expert"), None)
    return jax.shard_map(
        on_device,
        mesh=mesh,
        in_specs=(rows, rows, rows, rows, P("expert", None), P("expert", None, None), P("expert", None, None)),
        out_specs=(rows, rows, P("expert", None)),
        check_vma=False,
    )
```

time: 213 us -> 166 us (0.78)
  the two profiles are of different devices: /device:TPU:43 before, /device:TPU:7 now
where the time goes in v3:
time: 166 us
  Pallas kernels  159 us (96%)
  local copies, waits for them, and re-layouts  5.63 us (3%)
    pallas_call x1, Pallas kernels, on_device(): pl.pallas_call(kernel, out_shape=(jax.ShapeDtypeStruct((128, 4096), BF),...  159 us
    unnamed x3, local copies, waits for them, and re-layouts  5.63 us

profile of v3, /device:TPU:7, one launch (start us, length us, event | category | flops | bytes accessed | tf_op | source)
XLA Modules:
  0.0 165.6 jit_solution(732817293539872140)
XLA Ops:
  0.6 159.3 %moe_layer.1 = (bf16[128,4096]{1,0:T(8,128)(2,1)}, bf16[128,1024]{1,0:T(8,128)(2,1)}, f32[64,1024]{1,0:T(8,128)}) custom-call(bf16[128,1024]{1,0:T(8,128)(2,1)} %latent.1, s32[8,128]{1,0:T(8,128)} %bitcast.2, f32[8,128]{1,0:T(8,128)} %bitcast.3, bf16[64,1024]{1,0:T(8,128)(2,1)} %w_own.1, bf16[128,4096]{1,0:T(8,128)(2,1)} %grad_out.1, ...), custom_call_target="tpu_custom_call" | custom-call | flops 24999999488 | bytes 20000000 | tf_op jit(solution)/shard_map/moe_layer/pallas_call | solution.py:621
  160.0 2.3 %copy.13 = bf16[128,4096]{1,0:T(8,128)(2,1)} copy(bf16[128,4096]{1,0:T(8,128)(2,1)} %get-tuple-element.6) | data formatting | bytes 2097152
  162.3 1.7 %copy.14 = bf16[128,1024]{1,0:T(8,128)(2,1)} copy(bf16[128,1024]{1,0:T(8,128)(2,1)} %get-tuple-element.7) | data formatting | bytes 524288
  163.9 1.7 %copy.15 = f32[64,1024]{1,0:T(8,128)} copy(f32[64,1024]{1,0:T(8,128)} %get-tuple-element.8) | data formatting | bytes 524288

commit v4 on v3

--- a/solution.py
+++ b/solution.py
@@ -38,11 +38,11 @@
     mixed, grad_latent, grad_w,
     s1, r1, b1, s2, r2, b2, up, down, relu, xc, acc, extra,
     routes4, gates4, latent4, gc4, part_f, part_s, part_r,
-    go, wj, pga, pgb, pgs, pgr, cb, mps, gwp, gwy, gws, gwx, dps, dpr,
+    go, wj, pga, pgb, pgs, pgr, cb, mps, gwp, gwy, gws, gwx, gwb, gwbs, gwby, dps, dpr,
     slots, gate_tab, sel, selt, p_send, pg_send, p_back, pg_back,
-    a2a_ss, a2a_rs, grp_ss, grp_rs, sw_ss, sw_rs, wx_ss, wx_rs, wy_ss, wy_rs, go_ss, go_rs,
+    a2a_ss, a2a_rs, grp_ss, grp_rs, sw_ss, sw_rs, wx_ss, wx_rs, wb_ss, wb_rs, wbx_ss, wbx_rs, wy_ss, wy_rs, go_ss, go_rs,
     sib_ss, sib_rs, bgc_ss, bgc_rs, pg_ss, pg_rs, cb_ss, cb_rs, cf_ss, mx_ss, mx_rs,
-    gy_ss, gy_rs, gx_ss, gx_rs, dp_sem, loc,
+    gy_ss, gy_rs, gb_ss, gb_rs, gby_ss, gby_rs, gx_ss, gx_rs, dp_sem, loc,
 ):
     dp = lax.axis_index("dp")
     me = lax.axis_index("expert")
@@ -98,7 +98,8 @@
         near = (x * 2 + c + d) % 8
         signal(dp, index_of(y, z, near // 2, near % 2))
     for d in range(1, 4):
-        signal(dp, index_of((y + d) % 4, z, x, c))
+        for cc in range(2):
+            signal(dp, index_of((y + d) % 4, z, x, cc))
     up_copy = pltpu.make_async_copy(up_hbm.at[0], up, loc.at[0])
     down_copy = pltpu.make_async_copy(down_hbm.at[0], down, loc.at[1])
     up_copy.start()
@@ -112,7 +113,31 @@
     sel[...] = jnp.where(((i & 63) >> 2) * 16 + (i >> 6) * 4 + (i & 3) == j, 1.0, 0.0).astype(BF)
     selt[...] = jnp.where(((j & 63) >> 2) * 16 + (j >> 6) * 4 + (j & 3) == i, 1.0, 0.0).astype(BF)
 
-    pl.semaphore_wait(barrier, 47)
+    pl.semaphore_wait(barrier, 50)
+
+    sends_w = parity == (y + dp) % 2
+    w_slot = rows_at(y * 128 + c * 64, 64)
+
+    near_half, far_half = pl.ds(0, 512), pl.ds(512, 512)
+
+    def wx(d):
+        to = index_of(y, z, (x + d) % 4, half)
+        return to, remote(w_own.at[:, near_half], wj.at[w_slot, near_half], wx_ss.at[d], wx_rs.at[c], to)
+
+    def wb(d):
+        to = index_of((y + d) % 4, z, x, half)
+        return to, remote(w_own.at[:, far_half], wj.at[w_slot, far_half], wb_ss.at[d], wb_rs.at[y * 2 + c], to)
+
+    for d in (1, 3, 2, 0):
+        for to, copy in (wx(d), wb(d)):
+
+            @pl.when(jnp.logical_and(sends_w, to != me))
+            def _():
+                copy.start()
+
+    @pl.when(jnp.logical_and(sends_w, c == half))
+    def _():
+        wj[w_slot, :] = w_own[...]
 
     swap = []
     for d in (1, 3, 2):
@@ -129,27 +154,6 @@
         for d in (1, 3, 2):
             g, _ = group_at(d)
             remote(dst(g), dst(g), grp_ss.at[n, d], grp_rs.at[n, g], me).wait_recv()
-
-    sends_w = parity == (y + dp) % 2
-    w_slot = rows_at(y * 128 + c * 64, 64)
-
-    def wx(d):
-        to = index_of(y, z, (x + d) % 4, half)
-        return to, remote(w_own, wj.at[w_slot], wx_ss.at[d], wx_rs.at[c], to)
-
-    for d in (1, 3, 2, 0):
-        to, copy = wx(d)
-        go_on = jnp.logical_and(sends_w, to != me)
-
-        @pl.when(go_on)
-        def _():
-            copy.start()
-
-        if d == 0:
-
-            @pl.when(jnp.logical_and(sends_w, to == me))
-            def _():
-                wj[w_slot, :] = w_own[...]
 
     def feats(m, part):
         to = m % 4
@@ -259,7 +263,8 @@
 
         @pl.when(src != me)
         def _():
-            remote(w_own, wj.at[rows_at(y * 128 + cc * 64, 64)], wx_ss.at[0], wx_rs.at[cc], me).wait_recv()
+            piece = wj.at[rows_at(y * 128 + cc * 64, 64), near_half]
+            remote(piece, piece, wx_ss.at[0], wx_rs.at[cc], me).wait_recv()
 
     def along_y(d):
         py = (y + d) % 4
@@ -267,10 +272,36 @@
 
     def wy(d):
         _, to = along_y(d)
-        return remote(wj.at[tokens(y)], wj.at[tokens(y)], wy_ss.at[d], wy_rs.at[y], to)
+        piece = wj.at[tokens(y), near_half]
+        return remote(piece, piece, wy_ss.at[d], wy_rs.at[y], to)
 
     for d in (1, 3, 2):
         wy(d).start()
+
+    def own_y(n):
+        return (x + dp) % 2 + 2 * n
+
+    def wbx(n, d):
+        py = own_y(n)
+        piece = wj.at[tokens(py), far_half]
+        return remote(piece, piece, wbx_ss.at[n, d], wbx_rs.at[py], index_of(y, z, (x + d) % 4, c))
+
+    def far_source(py):
+        return 2 * c + (py + dp) % 2
+
+    @pl.when(c == half)
+    def _():
+        for n in range(2):
+            py = own_y(n)
+            for cc in range(2):
+
+                @pl.when(index_of(py, z, x, cc) != me)
+                def _():
+                    piece = wj.at[rows_at(py * 128 + cc * 64, 64), far_half]
+                    remote(piece, piece, wb_ss.at[0], wb_rs.at[py * 2 + cc], me).wait_recv()
+
+            for d in (1, 3, 2):
+                wbx(n, d).start()
 
     from_group(2, lambda g: latent4.at[rows_at(g * 128, 128)])
     dispatch(0, p_send, latent4, s1, r1)
@@ -342,7 +373,15 @@
     def gc_sibling():
         for d in (1, 3, 2):
             py, _ = along_y(d)
-            remote(wj.at[tokens(py)], wj.at[tokens(py)], wy_ss.at[d], wy_rs.at[py], me).wait_recv()
+            piece = wj.at[tokens(py), near_half]
+            remote(piece, piece, wy_ss.at[d], wy_rs.at[py], me).wait_recv()
+        for py in range(4):
+
+            @pl.when(x != far_source(py))
+            def _():
+                piece = wj.at[tokens(py), far_half]
+                remote(piece, piece, wbx_ss.at[0, 1], wbx_rs.at[py], me).wait_recv()
+
         for copy in own_go:
             copy.wait()
         for n, (dc, dz) in enumerate(others):
@@ -454,6 +493,14 @@
         src, dst = gwp.at[tokens(py), cols], gwy.at[tokens(y), cols]
         return py, remote(src, dst, gy_ss.at[d, q], gy_rs.at[y, q], to)
 
+    def far_cols(q):
+        return pl.ds(q * 256 - 512, 256)
+
+    def gb(py, q):
+        to = index_of(y, z, far_source(py), c)
+        src, dst = gwp.at[tokens(py), cols_of(q)], gwb.at[py // 2, tokens(x), far_cols(q)]
+        return to, remote(src, dst, gb_ss.at[py, q - 2], gb_rs.at[py // 2, x, q - 2], to)
+
     def weight_grad():
         for q in range(4):
             for d in range(4):
@@ -461,9 +508,21 @@
                 cb_copy(m, q, cb_ss.at[d, q], me, dp).wait_recv()
             cols = cols_of(q)
             gwp[:, cols] = dot(go[...], cb[:, cols], 0, 0).astype(BF)
-            for d in (1, 3, 2):
-                gy(d, q)[1].start()
-            gwy[tokens(y), cols] = gwp[tokens(y), cols]
+            if q < 2:
+                for d in (1, 3, 2):
+                    gy(d, q)[1].start()
+                gwy[tokens(y), cols] = gwp[tokens(y), cols]
+            else:
+                for py in range(4):
+                    to, copy = gb(py, q)
+
+                    @pl.when(to != me)
+                    def _():
+                        copy.start()
+
+                    @pl.when(to == me)
+                    def _():
+                        gwb[py // 2, tokens(x), far_cols(q)] = gwp[tokens(py), cols]
 
     def mix_all():
         def mix(part, carry):
@@ -483,27 +542,27 @@
     gc_sibling()
     gc_ring()
     forward(0)
+    forward(1)
+    forward(2)
     gc_swap()
-    forward(1)
+    forward(3)
     gc_dispatch()
-    forward(2)
-    forward(3)
     backward(0)
     backward(1)
     combine()
     backward(2)
+    backward(3)
     share_start()
-    backward(3)
     share_pass()
     weight_grad()
     mix_all()
 
-    for q in range(4):
+    for q in range(2):
         for d in (1, 3, 2):
             py, _ = along_y(d)
             piece = gwy.at[tokens(py), cols_of(q)]
             remote(piece, piece, gy_ss.at[d, q], gy_rs.at[py, q], me).wait_recv()
-    gws[...] = sum(gwy[n * 128 : (n + 1) * 128, :].astype(F32) for n in range(4)).astype(BF)
+    gws[...] = sum(gwy[n * 128 : (n + 1) * 128, 0:512].astype(F32) for n in range(4)).astype(BF)
     x_slot = rows_at(x * 64, 64)
 
     def gx(cc):
@@ -520,6 +579,35 @@
         @pl.when(to == me)
         def _():
             gwx[x_slot, :] = gws[cc * 64 : cc * 64 + 64, :]
+
+    def gby(n, cc):
+        to = index_of(own_y(n), z, x, cc)
+        src = gwbs.at[n, pl.ds(cc * 64, 64)]
+        return to, remote(src, gwby.at[rows_at(y * 64, 64)], gby_ss.at[n, cc], gby_rs.at[y], to)
+
+    @pl.when(c == half)
+    def _():
+        for n in range(2):
+            for px in range(4):
+
+                @pl.when(x != px)
+                def _():
+                    for q in range(2):
+                        piece = gwb.at[n, pl.ds(px * 128, 128), cols_of(q)]
+                        remote(piece, piece, gb_ss.at[0, q], gb_rs.at[n, px, q], me).wait_recv()
+
+            gwbs[n] = sum(gwb[n, px * 128 : px * 128 + 128, :].astype(F32) for px in range(4)).astype(BF)
+            for cc in range(2):
+                to, copy = gby(n, cc)
+
+                @pl.when(to != me)
+                def _():
+                    copy.start()
+
+                @pl.when(to == me)
+                def _():
+                    gwby[rows_at(y * 64, 64), :] = gwbs[n, cc * 64 : cc * 64 + 64, :]
+
 
     gather_back(3, r2, b2)
     part_sums(1, p_back, b2)
@@ -538,7 +626,15 @@
                 rows = pl.ds(px * 64, 64)
                 remote(gwx.at[rows], gwx.at[rows], gx_ss.at[0], gx_rs.at[px], me).wait_recv()
 
-        dps[...] = sum(gwx[n * 64 : (n + 1) * 64, :].astype(F32) for n in range(4)).astype(BF)
+        for py in range(4):
+
+            @pl.when(index_of(py, z, x, half) != me)
+            def _():
+                rows = pl.ds(py * 64, 64)
+                remote(gwby.at[rows], gwby.at[rows], gby_ss.at[0, 0], gby_rs.at[py], me).wait_recv()
+
+        dps[:, 0:512] = sum(gwx[n * 64 : (n + 1) * 64, :].astype(F32) for n in range(4)).astype(BF)
+        dps[:, 512:1024] = sum(gwby[n * 64 : (n + 1) * 64, :].astype(F32) for n in range(4)).astype(BF)
         exchange.start()
         grad_w[...] = dps[...].astype(F32)
 
@@ -563,17 +659,24 @@
     for copy in swap + swap_gc + to_sibling:
         copy.wait_send()
     for d in range(4):
-        to, copy = wx(d)
-        go_on = jnp.logical_and(sends_w, to != me)
-
-        @pl.when(go_on)
-        def _():
-            copy.wait_send()
+        for to, copy in (wx(d), wb(d)):
+
+            @pl.when(jnp.logical_and(sends_w, to != me))
+            def _():
+                copy.wait_send()
+
+        for q in range(2):
+            to, copy = gb(d, q + 2)
+
+            @pl.when(to != me)
+            def _():
+                copy.wait_send()
 
         for q in range(4):
             cb_copy(mine, q, cb_ss.at[d, q], me, dp).wait_send()
             if d:
-                gy(d, q)[1].wait_send()
+                if q < 2:
+                    gy(d, q)[1].wait_send()
                 cb_copy(mine, q, cf_ss.at[d, q], me, dp).wait_send()
         if d:
             wy(d).wait_send()
@@ -581,6 +684,18 @@
                 pg_copy(d, q).wait_send()
                 part_copy(0, d, q).wait_send()
                 part_copy(1, d, q).wait_send()
+    @pl.when(c == half)
+    def _():
+        for n in range(2):
+            for d in (1, 2, 3):
+                wbx(n, d).wait_send()
+            for cc in range(2):
+                to, copy = gby(n, cc)
+
+                @pl.when(to != me)
+                def _():
+                    copy.wait_send()
+
     for cc in range(2):
         to, copy = gx(cc)
 
@@ -592,6 +707,15 @@
     all_sent(1, r1, b1)
     all_sent(2, s2, r2)
     all_sent(3, r2, b2)
+
+
+def settle(mixed_in, latent_in, w_in, mixed, grad_latent, grad_w, sems):
+    pairs = ((mixed_in, mixed), (latent_in, grad_latent), (w_in, grad_w))
+    copies = [pltpu.make_async_copy(src, dst, sems.at[n]) for n, (src, dst) in enumerate(pairs)]
+    for copy in copies:
+        copy.start()
+    for copy in copies:
+        copy.wait()
 
 
 def on_device(latent, routes, gates, grad_out, w_out_t, expert_up, expert_down):
@@ -610,21 +734,22 @@
         pltpu.VMEM((4, 8, 128), I32), pltpu.VMEM((4, 8, 128), F32), bf(512, 1024), bf(512, 1024),
         pltpu.VMEM((512, 1024), F32), bf(2, 4, 128, 1024), bf(2, 4, 128, 1024),
         bf(1024, 512), bf(512, 1024), bf(512, 1024), bf(512, 1024), bf(512, 1024), bf(512, 1024),
-        bf(1024, 1024), bf(1024, 512), bf(512, 1024), bf(512, 1024), bf(128, 1024), bf(256, 1024),
+        bf(1024, 1024), bf(1024, 512), bf(512, 1024), bf(512, 512), bf(128, 512), bf(256, 512), bf(2, 512, 512), bf(2, 128, 512), bf(256, 512),
         bf(64, 1024), bf(64, 1024),
         pltpu.VMEM((4, 128, 128), F32), pltpu.VMEM((4, 128, 128), F32), bf(256, 256), bf(256, 256),
         bf(4, 320, 128), bf(4, 320, 256), bf(4, 128, 320), bf(4, 256, 320),
-        dma(4), dma(4, 4), dma(3, 4), dma(3, 4), dma(2, 4, 4), dma(2, 4, 4), dma(4), dma(2), dma(4), dma(4), dma(7), dma(8),
+        dma(4), dma(4, 4), dma(3, 4), dma(3, 4), dma(2, 4, 4), dma(2, 4, 4), dma(4), dma(2), dma(4), dma(8), dma(2, 4), dma(4), dma(4), dma(4), dma(7), dma(8),
         dma(4), dma(4), dma(4, 4), dma(4, 4), dma(4, 4), dma(4, 4), dma(4, 4), dma(8, 4), dma(4, 4), dma(7), dma(8),
-        dma(4, 4), dma(4, 4), dma(2), dma(4), dma(2), dma(6),
+        dma(4, 4), dma(4, 4), dma(4, 2), dma(2, 4, 2), dma(2, 2), dma(4), dma(2), dma(4), dma(2), dma(6),
     ]
-    return pl.pallas_call(
+    shapes = (
+        jax.ShapeDtypeStruct((128, 4096), BF),
+        jax.ShapeDtypeStruct((128, 1024), BF),
+        jax.ShapeDtypeStruct((64, 1024), F32),
+    )
+    results = pl.pallas_call(
         kernel,
-        out_shape=(
-            jax.ShapeDtypeStruct((128, 4096), BF),
-            jax.ShapeDtypeStruct((128, 1024), BF),
-            jax.ShapeDtypeStruct((64, 1024), F32),
-        ),
+        out_shape=shapes,
         in_specs=[vm, vm, vm, vm, hbm, hbm, hbm],
         out_specs=(vm, vm, vm),
         scratch_shapes=scratch,
@@ -634,6 +759,14 @@
         cost_estimate=pl.CostEstimate(flops=25_000_000_000, bytes_accessed=20_000_000, transcendentals=0),
         name="moe_layer",
     )(latent, routes.T, gates.T, w_out_t, grad_out, expert_up, expert_down)
+    return pl.pallas_call(
+        settle,
+        out_shape=shapes,
+        in_specs=[vm] * 3,
+        out_specs=(hbm,) * 3,
+        scratch_shapes=[dma(3)],
+        name="settle",
+    )(*results)
 
 
 def solution(mesh):

time: 166 us -> 145 us (0.87); the launches traced: 166 us -> 142 us
  Pallas kernels: 159 us -> 141 us
  local copies, waits for them, and re-layouts: 5.63 us -> 0 us
    pallas_call x1 -> x2, Pallas kernels: 159 us -> 141 us  [the longest x1 139 us: on_device(): pl.pallas_call(kernel, out_shape=shapes, in_specs=[vm, vm, vm, vm, hbm, h...]
    unnamed x3 -> x0, local copies, waits for them, and re-layouts: 5.63 us -> none
where the time goes in v4:
time: 145 us; the launch traced here: 142 us
  Pallas kernels  141 us (97%)
    pallas_call x1, Pallas kernels, on_device(): pl.pallas_call(kernel, out_shape=shapes, in_specs=[vm, vm, vm, vm, hbm, h...  139 us

profile of v4, /device:TPU:7, one launch (start us, length us, event | category | flops | bytes accessed | tf_op | source)
XLA Modules:
  0.0 142.3 jit_solution(10334420618688167433)
XLA Ops:
  0.6 139.0 %moe_layer.1 = (bf16[128,4096]{1,0:T(8,128)(2,1)}, bf16[128,1024]{1,0:T(8,128)(2,1)}, f32[64,1024]{1,0:T(8,128)}) custom-call(bf16[128,1024]{1,0:T(8,128)(2,1)} %latent.1, s32[8,128]{1,0:T(8,128)} %bitcast.2, f32[8,128]{1,0:T(8,128)} %bitcast.3, bf16[64,1024]{1,0:T(8,128)(2,1)} %w_own.1, bf16[128,4096]{1,0:T(8,128)(2,1)} %grad_out.1, ...), custom_call_target="tpu_custom_call" | custom-call | flops 24999999488 | bytes 20000000 | tf_op jit(solution)/shard_map/moe_layer/pallas_call | solution.py:750
  139.6 2.5 %settle.1 = (bf16[128,4096]{1,0:T(8,128)(2,1)}, bf16[128,1024]{1,0:T(8,128)(2,1)}, f32[64,1024]{1,0:T(8,128)}) custom-call(bf16[128,4096]{1,0:T(8,128)(2,1)} %get-tuple-element.6.mixed_in, bf16[128,1024]{1,0:T(8,128)(2,1)} %get-tuple-element.7.latent_in, f32[64,1024]{1,0:T(8,128)} %get-tuple-element.8.w_in), custom_call_target="tpu_custom_call" | custom-call | tf_op jit(solution)/shard_map/settle/pallas_call | solution.py:762

commit v5 on v4

--- a/solution.py
+++ b/solution.py
@@ -468,6 +468,10 @@
         gather_back(1, r1, b1)
         part_sums(0, pg_back, b1)
 
+    def combine_back():
+        gather_back(3, r2, b2)
+        part_sums(1, p_back, b2)
+
     def cb_copy(m, q, ss, dev, rep):
         piece = cb.at[tokens(m), cols_of(q)]
         return remote(piece, piece, ss, cb_rs.at[m, q], dev, rep)
@@ -547,15 +551,16 @@
     gc_swap()
     forward(3)
     gc_dispatch()
+    combine()
     backward(0)
+    share_start()
     backward(1)
-    combine()
     backward(2)
+    share_pass()
     backward(3)
-    share_start()
-    share_pass()
     weight_grad()
     mix_all()
+    combine_back()
 
     for q in range(2):
         for d in (1, 3, 2):
@@ -608,9 +613,6 @@
                 def _():
                     gwby[rows_at(y * 64, 64), :] = gwbs[n, cc * 64 : cc * 64 + 64, :]
 
-
-    gather_back(3, r2, b2)
-    part_sums(1, p_back, b2)
 
     exchange = pltpu.make_async_remote_copy(
         dps, dpr, dp_sem.at[0], dp_sem.at[1], device_id=(1 - dp, me), device_id_type=MESH

time: 145 us -> 141 us (0.972); the launches traced: 142 us -> 140 us
  Pallas kernels: 141 us -> 139 us
    pallas_call x1, Pallas kernels: 139 us -> 137 us  [on_device(): pl.pallas_call(kernel, out_shape=shapes, in_specs=[vm, vm, vm, vm, hbm, h...]
where the time goes in v5:
time: 141 us; the launch traced here: 140 us
  Pallas kernels  139 us (99%)
    pallas_call x1, Pallas kernels, on_device(): pl.pallas_call(kernel, out_shape=shapes, in_specs=[vm, vm, vm, vm, hbm, h...  137 us

profile of v5, /device:TPU:7, one launch (start us, length us, event | category | flops | bytes accessed | tf_op | source)
XLA Modules:
  0.0 140.0 jit_solution(506076039176296111)
XLA Ops:
  0.6 136.7 %moe_layer.1 = (bf16[128,4096]{1,0:T(8,128)(2,1)}, bf16[128,1024]{1,0:T(8,128)(2,1)}, f32[64,1024]{1,0:T(8,128)}) custom-call(bf16[128,1024]{1,0:T(8,128)(2,1)} %latent.1, s32[8,128]{1,0:T(8,128)} %bitcast.2, f32[8,128]{1,0:T(8,128)} %bitcast.3, bf16[64,1024]{1,0:T(8,128)(2,1)} %w_own.1, bf16[128,4096]{1,0:T(8,128)(2,1)} %grad_out.1, ...), custom_call_target="tpu_custom_call" | custom-call | flops 24999999488 | bytes 20000000 | tf_op jit(solution)/shard_map/moe_layer/pallas_call | solution.py:752
  137.3 2.5 %settle.1 = (bf16[128,4096]{1,0:T(8,128)(2,1)}, bf16[128,1024]{1,0:T(8,128)(2,1)}, f32[64,1024]{1,0:T(8,128)}) custom-call(bf16[128,4096]{1,0:T(8,128)(2,1)} %get-tuple-element.6.mixed_in, bf16[128,1024]{1,0:T(8,128)(2,1)} %get-tuple-element.7.latent_in, f32[64,1024]{1,0:T(8,128)} %get-tuple-element.8.w_in), custom_call_target="tpu_custom_call" | custom-call | tf_op jit(solution)/shard_map/settle/pallas_call | solution.py:764

commit v6 on v5

--- a/solution.py
+++ b/solution.py
@@ -556,8 +556,8 @@
     share_start()
     backward(1)
     backward(2)
+    backward(3)
     share_pass()
-    backward(3)
     weight_grad()
     mix_all()
     combine_back()

time: 141 us -> 139 us (0.986)
  Pallas kernels: 139 us -> 136 us
    pallas_call x1, Pallas kernels: 137 us -> 133 us  [on_device(): pl.pallas_call(kernel, out_shape=shapes, in_specs=[vm, vm, vm, vm, hbm, h...]
where the time goes in v6:
time: 139 us; the launch traced here: 137 us
  Pallas kernels  136 us (98%)
    pallas_call x1, Pallas kernels, on_device(): pl.pallas_call(kernel, out_shape=shapes, in_specs=[vm, vm, vm, vm, hbm, h...  133 us

profile of v6, /device:TPU:7, one launch (start us, length us, event | category | flops | bytes accessed | tf_op | source)
XLA Modules:
  0.0 136.7 jit_solution(16645991701626645855)
XLA Ops:
  0.6 133.3 %moe_layer.1 = (bf16[128,4096]{1,0:T(8,128)(2,1)}, bf16[128,1024]{1,0:T(8,128)(2,1)}, f32[64,1024]{1,0:T(8,128)}) custom-call(bf16[128,1024]{1,0:T(8,128)(2,1)} %latent.1, s32[8,128]{1,0:T(8,128)} %bitcast.2, f32[8,128]{1,0:T(8,128)} %bitcast.3, bf16[64,1024]{1,0:T(8,128)(2,1)} %w_own.1, bf16[128,4096]{1,0:T(8,128)(2,1)} %grad_out.1, ...), custom_call_target="tpu_custom_call" | custom-call | flops 24999999488 | bytes 20000000 | tf_op jit(solution)/shard_map/moe_layer/pallas_call | solution.py:752
  134.0 2.5 %settle.1 = (bf16[128,4096]{1,0:T(8,128)(2,1)}, bf16[128,1024]{1,0:T(8,128)(2,1)}, f32[64,1024]{1,0:T(8,128)}) custom-call(bf16[128,4096]{1,0:T(8,128)(2,1)} %get-tuple-element.6.mixed_in, bf16[128,1024]{1,0:T(8,128)(2,1)} %get-tuple-element.7.latent_in, f32[64,1024]{1,0:T(8,128)} %get-tuple-element.8.w_in), custom_call_target="tpu_custom_call" | custom-call | tf_op jit(solution)/shard_map/settle/pallas_call | solution.py:764

commit v7 on v6

--- a/solution.py
+++ b/solution.py
@@ -614,9 +614,10 @@
                     gwby[rows_at(y * 64, 64), :] = gwbs[n, cc * 64 : cc * 64 + 64, :]
 
 
-    exchange = pltpu.make_async_remote_copy(
-        dps, dpr, dp_sem.at[0], dp_sem.at[1], device_id=(1 - dp, me), device_id_type=MESH
-    )
+    exchange = []
+    for n, cols in enumerate((near_half, far_half)):
+        src, dst = dps.at[:, cols], dpr.at[:, cols]
+        exchange.append(remote(src, dst, dp_sem.at[n], dp_sem.at[2 + n], me, 1 - dp))
 
     @pl.when(sends_w)
     def _():
@@ -628,6 +629,8 @@
                 rows = pl.ds(px * 64, 64)
                 remote(gwx.at[rows], gwx.at[rows], gx_ss.at[0], gx_rs.at[px], me).wait_recv()
 
+        dps[:, 0:512] = sum(gwx[n * 64 : (n + 1) * 64, :].astype(F32) for n in range(4)).astype(BF)
+        exchange[0].start()
         for py in range(4):
 
             @pl.when(index_of(py, z, x, half) != me)
@@ -635,9 +638,8 @@
                 rows = pl.ds(py * 64, 64)
                 remote(gwby.at[rows], gwby.at[rows], gby_ss.at[0, 0], gby_rs.at[py], me).wait_recv()
 
-        dps[:, 0:512] = sum(gwx[n * 64 : (n + 1) * 64, :].astype(F32) for n in range(4)).astype(BF)
         dps[:, 512:1024] = sum(gwby[n * 64 : (n + 1) * 64, :].astype(F32) for n in range(4)).astype(BF)
-        exchange.start()
+        exchange[1].start()
         grad_w[...] = dps[...].astype(F32)
 
     for q in range(4):
@@ -645,11 +647,13 @@
 
     @pl.when(sends_w)
     def _():
-        exchange.wait_send()
+        for copy in exchange:
+            copy.wait_send()
 
     @pl.when(jnp.logical_not(sends_w))
     def _():
-        exchange.wait_recv()
+        for copy in exchange:
+            copy.wait_recv()
         grad_w[...] = dpr[...].astype(F32)
 
     for n, (dc, dz) in enumerate(others):
@@ -742,7 +746,7 @@
         bf(4, 320, 128), bf(4, 320, 256), bf(4, 128, 320), bf(4, 256, 320),
         dma(4), dma(4, 4), dma(3, 4), dma(3, 4), dma(2, 4, 4), dma(2, 4, 4), dma(4), dma(2), dma(4), dma(8), dma(2, 4), dma(4), dma(4), dma(4), dma(7), dma(8),
         dma(4), dma(4), dma(4, 4), dma(4, 4), dma(4, 4), dma(4, 4), dma(4, 4), dma(8, 4), dma(4, 4), dma(7), dma(8),
-        dma(4, 4), dma(4, 4), dma(4, 2), dma(2, 4, 2), dma(2, 2), dma(4), dma(2), dma(4), dma(2), dma(6),
+        dma(4, 4), dma(4, 4), dma(4, 2), dma(2, 4, 2), dma(2, 2), dma(4), dma(2), dma(4), dma(4), dma(6),
     ]
     shapes = (
         jax.ShapeDtypeStruct((128, 4096), BF),

time: 139 us -> 139 us (level)
  the two profiles are of different devices: /device:TPU:7 before, /device:TPU:41 now
where the time goes in v7:
time: 139 us
  Pallas kernels  138 us (99%)
    pallas_call x1, Pallas kernels, on_device(): pl.pallas_call(kernel, out_shape=shapes, in_specs=[vm, vm, vm, vm, hbm, h...  135 us

profile of v7, /device:TPU:41, one launch (start us, length us, event | category | flops | bytes accessed | tf_op | source)
XLA Modules:
  0.0 138.8 jit_solution(7630676355718060786)
XLA Ops:
  0.6 135.4 %moe_layer.1 = (bf16[128,4096]{1,0:T(8,128)(2,1)}, bf16[128,1024]{1,0:T(8,128)(2,1)}, f32[64,1024]{1,0:T(8,128)}) custom-call(bf16[128,1024]{1,0:T(8,128)(2,1)} %latent.1, s32[8,128]{1,0:T(8,128)} %bitcast.2, f32[8,128]{1,0:T(8,128)} %bitcast.3, bf16[64,1024]{1,0:T(8,128)(2,1)} %w_own.1, bf16[128,4096]{1,0:T(8,128)(2,1)} %grad_out.1, ...), custom_call_target="tpu_custom_call" | custom-call | flops 24999999488 | bytes 20000000 | tf_op jit(solution)/shard_map/moe_layer/pallas_call | solution.py:756
  136.1 2.5 %settle.1 = (bf16[128,4096]{1,0:T(8,128)(2,1)}, bf16[128,1024]{1,0:T(8,128)(2,1)}, f32[64,1024]{1,0:T(8,128)}) custom-call(bf16[128,4096]{1,0:T(8,128)(2,1)} %get-tuple-element.6.mixed_in, bf16[128,1024]{1,0:T(8,128)(2,1)} %get-tuple-element.7.latent_in, f32[64,1024]{1,0:T(8,128)} %get-tuple-element.8.w_in), custom_call_target="tpu_custom_call" | custom-call | tf_op jit(solution)/shard_map/settle/pallas_call | solution.py:768
